TPU v7x, 32 devices: a whole 2x2x4 slice. The times are simulated.
32 devices in a mesh: replica: 2 (over x), fsdp: 16 (over z, y, core).
Axes of the slice: x: 2, y: 2, z: 4, core: 2. Of those that a mesh axis runs over, the one named last changes fastest.
Arguments:
- layer_in: bfloat16 [8192, 1152], P(('replica', 'fsdp')), may hold values from -6 to 6
- d_out: bfloat16 [8192, 1152], P(('replica', 'fsdp')), may hold values from -6 to 6
- segments: int32 [32, 256], P(('replica', 'fsdp')), may hold values from 0 to 255, as said below
- w_q: float32 [1152, 1024], P('fsdp'), may hold values from -0.1875 to 0.1875
- w_k: float32 [1152, 256], P('fsdp'), may hold values from -0.1875 to 0.1875
- w_v: float32 [1152, 256], P('fsdp'), may hold values from -0.1875 to 0.1875
- w_o: float32 [1024, 1152], P('fsdp'), may hold values from -0.1875 to 0.1875
- attn_pre: float32 [1152], P('fsdp'), may hold values from 0.5 to 1.5
- attn_post: float32 [1152], P('fsdp'), may hold values from 0.5 to 1.5
- q_gain: float32 [256], P('fsdp'), may hold values from 0.5 to 1.5
- k_gain: float32 [256], P('fsdp'), may hold values from 0.5 to 1.5
- w_gate: float32 [1152, 6912], P('fsdp'), may hold values from -0.1875 to 0.1875
- w_up: float32 [1152, 6912], P('fsdp'), may hold values from -0.1875 to 0.1875
- w_down: float32 [6912, 1152], P('fsdp'), may hold values from -0.078125 to 0.078125
- mlp_pre: float32 [1152], P('fsdp'), may hold values from 0.5 to 1.5
- mlp_post: float32 [1152], P('fsdp'), may hold values from 0.5 to 1.5
Outputs:
- layer_out: bfloat16 [8192, 1152], P(('replica', 'fsdp'))
- grad_x: bfloat16 [8192, 1152], P(('replica', 'fsdp'))
- grad_w_q: float32 [1152, 1024], P('fsdp')
- grad_w_k: float32 [1152, 256], P('fsdp')
- grad_w_v: float32 [1152, 256], P('fsdp')
- grad_w_o: float32 [1024, 1152], P('fsdp')
- grad_attn_pre: float32 [1152], P('fsdp')
- grad_attn_post: float32 [1152], P('fsdp')
- grad_q_gain: float32 [256], P('fsdp')
- grad_k_gain: float32 [256], P('fsdp')
- grad_w_gate: float32 [1152, 6912], P('fsdp')
- grad_w_up: float32 [1152, 6912], P('fsdp')
- grad_w_down: float32 [6912, 1152], P('fsdp')
- grad_mlp_pre: float32 [1152], P('fsdp')
- grad_mlp_post: float32 [1152], P('fsdp')
Inputs may be any that keep to these rules, and one draw needn't show every extreme that they name: `segments`: within each sequence the numbers start at 0 and rise by 0 or 1 from one token to the next; tokens with one number form a document. The first sequence holds a single document; the last often holds a document for every token.
All inputs are finite; a program needn't handle non-finite values.
Results may differ from a plain program's by a relative error of at most 0.018.
The roundings to bfloat16 on the way count: a program that leaves them out, or rounds other values in their place, can miss the bound.
Values may be sent and summed in bfloat16 or wider, within the bound.
A program may use at most 256 MiB of HBM per device.

v0:
```python
from functools import partial
import math

import jax
import jax.numpy as jnp
from jax import lax
from jax.sharding import PartitionSpec as P

EPS = 1e-06
THETA = 1000000.0
SCALE = 0.0625
MASKED = -1e30


def norm_rows(values, gain):
    return values * lax.rsqrt(jnp.mean(values * values, axis=-1, keepdims=True) + EPS) * gain


def positions_of(segments):
    length = segments.shape[-1]
    index = jnp.arange(length, dtype=jnp.int32)
    earlier = jnp.concatenate([segments[:, :1] - 1, segments[:, :-1]], axis=1)
    starts = jnp.where(segments != earlier, index[None, :], jnp.zeros_like(segments))
    return index[None, :] - lax.cummax(starts, axis=1)


def angle_tables(segments, head_size):
    half_size = head_size // 2
    rates = jnp.exp(jnp.arange(half_size, dtype=jnp.float32) * (-2.0 * math.log(THETA) / head_size))
    angles = positions_of(segments).astype(jnp.float32)[..., None] * rates
    return (jnp.cos(angles), jnp.sin(angles))


def rotate(values, cosine, sine):
    half_size = values.shape[-1] // 2
    first_half = values[..., :half_size]
    second_half = values[..., half_size:]
    return jnp.concatenate(
        [first_half * cosine - second_half * sine, second_half * cosine + first_half * sine],
        axis=-1,
    )


def query_path(projected, gain, cosine, sine):
    shaped = projected.reshape(projected.shape[0], projected.shape[1], -1, gain.shape[0])
    return rotate(norm_rows(shaped, gain), cosine[:, :, None, :], sine[:, :, None, :])


def key_path(projected, gain, cosine, sine):
    return rotate(norm_rows(projected, gain), cosine, sine)


def gelu_product(gate_val, up_val):
    return jax.nn.gelu(gate_val, approximate=True) * up_val


def to_low(values):
    return values.astype(jnp.bfloat16)


def matmul(left, right):
    return jnp.dot(left, right, preferred_element_type=jnp.float32)


def matmul_left_t(left, right):
    return lax.dot_general(
        left, right, (((0,), (0,)), ((), ())), preferred_element_type=jnp.float32
    )


def matmul_right_t(left, right):
    return lax.dot_general(
        left, right, (((1,), (1,)), ((), ())), preferred_element_type=jnp.float32
    )


def attention_masks(segments):
    length = segments.shape[1]
    index = jnp.arange(length, dtype=jnp.int32)
    causal = index[None, :] <= index[:, None]
    return (segments[:, :, None] == segments[:, None, :]) & causal[None]


def scores_of(q_low, k_low, masks):
    scores = SCALE * jnp.einsum("nqhd,nkd->nhqk", q_low, k_low, preferred_element_type=jnp.float32)
    return jnp.where(masks[:, None], scores, MASKED)


def spread_gain(values):
    return jnp.broadcast_to(values[:, None], (values.shape[0], lax.axis_size("replica")))


def body(
    layer_in,
    d_out,
    segments,
    w_q,
    w_k,
    w_v,
    w_o,
    attn_pre,
    attn_post,
    q_gain,
    k_gain,
    w_gate,
    w_up,
    w_down,
    mlp_pre,
    mlp_post,
):
    attn_set = (
        lax.all_gather(to_low(w_q), "fsdp", axis=0, tiled=True),
        lax.all_gather(to_low(w_k), "fsdp", axis=0, tiled=True),
        lax.all_gather(to_low(w_v), "fsdp", axis=0, tiled=True),
        lax.all_gather(to_low(w_o), "fsdp", axis=0, tiled=True),
        lax.all_gather(to_low(attn_pre), "fsdp", axis=0, tiled=True),
        lax.all_gather(to_low(attn_post), "fsdp", axis=0, tiled=True),
        lax.all_gather(to_low(q_gain), "fsdp", axis=0, tiled=True),
        lax.all_gather(to_low(k_gain), "fsdp", axis=0, tiled=True),
    )
    q_full, k_full, v_full, o_full = (attn_set[0], attn_set[1], attn_set[2], attn_set[3])
    gain_apre = attn_set[4].astype(jnp.float32)
    gain_apost = attn_set[5].astype(jnp.float32)
    gain_q = attn_set[6].astype(jnp.float32)
    gain_k = attn_set[7].astype(jnp.float32)
    mlp_set = (
        lax.all_gather(to_low(w_gate), "fsdp", axis=0, tiled=True),
        lax.all_gather(to_low(w_up), "fsdp", axis=0, tiled=True),
        lax.all_gather(to_low(w_down), "fsdp", axis=0, tiled=True),
        lax.all_gather(to_low(mlp_pre), "fsdp", axis=0, tiled=True),
        lax.all_gather(to_low(mlp_post), "fsdp", axis=0, tiled=True),
    )
    gate_full, up_full, down_full = (mlp_set[0], mlp_set[1], mlp_set[2])
    gain_mpre = mlp_set[3].astype(jnp.float32)
    gain_mpost = mlp_set[4].astype(jnp.float32)
    seq_count, seq_len = segments.shape
    tok_flat = layer_in.astype(jnp.float32)
    cosine, sine = angle_tables(segments, gain_q.shape[0])
    masks = attention_masks(segments)
    normed_a, pull_a = jax.vjp(norm_rows, tok_flat, gain_apre)
    a_low = to_low(normed_a)
    q_proj = matmul(a_low, q_full).reshape(seq_count, seq_len, -1)
    k_proj = matmul(a_low, k_full).reshape(seq_count, seq_len, -1)
    v_proj = matmul(a_low, v_full)
    q_rot, pull_q = jax.vjp(partial(query_path, cosine=cosine, sine=sine), q_proj, gain_q)
    k_rot, pull_k = jax.vjp(partial(key_path, cosine=cosine, sine=sine), k_proj, gain_k)
    q_low = to_low(q_rot)
    k_low = to_low(k_rot)
    v_low = to_low(v_proj).reshape(seq_count, seq_len, -1)
    scores = scores_of(q_low, k_low, masks)
    top_val = jnp.max(scores, axis=-1, keepdims=True)
    log_total = top_val + jnp.log(jnp.sum(jnp.exp(scores - top_val), axis=-1, keepdims=True))
    p_low = to_low(jnp.exp(scores - log_total))
    attn_mix = jnp.einsum("nhqk,nkd->nqhd", p_low, v_low, preferred_element_type=jnp.float32)
    o_low = to_low(attn_mix.reshape(seq_count * seq_len, -1))
    attn_proj = matmul(o_low, o_full)
    post_attn, pull_pa = jax.vjp(norm_rows, attn_proj, gain_apost)
    h_mid = tok_flat + post_attn
    normed_m, pull_m = jax.vjp(norm_rows, h_mid, gain_mpre)
    m_low = to_low(normed_m)
    gate_val = matmul(m_low, gate_full)
    up_val = matmul(m_low, up_full)
    hidden, pull_h = jax.vjp(gelu_product, gate_val, up_val)
    h_low = to_low(hidden)
    down_val = matmul(h_low, down_full)
    post_mlp, pull_pm = jax.vjp(norm_rows, down_val, gain_mpost)
    layer_out = (h_mid + post_mlp).astype(jnp.bfloat16)
    gate_full, up_full, down_full = (
        lax.all_gather(to_low(w_gate), "fsdp", axis=0, tiled=True),
        lax.all_gather(to_low(w_up), "fsdp", axis=0, tiled=True),
        lax.all_gather(to_low(w_down), "fsdp", axis=0, tiled=True),
    )
    grad_top = d_out.astype(jnp.float32)
    d_down, grad_mpost = pull_pm(grad_top)
    d_down_low = to_low(d_down)
    grad_wdown = matmul_left_t(h_low, d_down_low)
    d_hidden = matmul_right_t(d_down_low, down_full)
    d_gate, d_up = pull_h(d_hidden)
    d_gate_low = to_low(d_gate)
    d_up_low = to_low(d_up)
    grad_wgate = matmul_left_t(m_low, d_gate_low)
    grad_wup = matmul_left_t(m_low, d_up_low)
    d_normed = matmul_right_t(d_gate_low, gate_full) + matmul_right_t(d_up_low, up_full)
    d_mid_norm, grad_mpre = pull_m(d_normed)
    d_mid = grad_top + d_mid_norm
    q_full, k_full, v_full, o_full = (
        lax.all_gather(to_low(w_q), "fsdp", axis=0, tiled=True),
        lax.all_gather(to_low(w_k), "fsdp", axis=0, tiled=True),
        lax.all_gather(to_low(w_v), "fsdp", axis=0, tiled=True),
        lax.all_gather(to_low(w_o), "fsdp", axis=0, tiled=True),
    )
    d_attn, grad_apost = pull_pa(d_mid)
    d_attn_low = to_low(d_attn)
    grad_wo = matmul_left_t(o_low, d_attn_low)
    d_mix_low = to_low(matmul_right_t(d_attn_low, o_full)).reshape(
        seq_count, seq_len, -1, k_low.shape[-1]
    )
    probs = jnp.exp(scores_of(q_low, k_low, masks) - log_total)
    d_probs = jnp.einsum("nqhd,nkd->nhqk", d_mix_low, v_low, preferred_element_type=jnp.float32)
    row_dot = jnp.sum(probs * d_probs, axis=-1, keepdims=True)
    d_scores_low = to_low(probs * (d_probs - row_dot))
    d_query = SCALE * jnp.einsum(
        "nhqk,nkd->nqhd", d_scores_low, k_low, preferred_element_type=jnp.float32
    )
    d_key = SCALE * jnp.einsum(
        "nhqk,nqhd->nkd", d_scores_low, q_low, preferred_element_type=jnp.float32
    )
    d_value = jnp.einsum("nhqk,nqhd->nkd", p_low, d_mix_low, preferred_element_type=jnp.float32)
    d_qproj, grad_qgain = pull_q(d_query)
    d_kproj, grad_kgain = pull_k(d_key)
    d_q_low = to_low(d_qproj.reshape(seq_count * seq_len, -1))
    d_k_low = to_low(d_kproj.reshape(seq_count * seq_len, -1))
    d_v_low = to_low(d_value.reshape(seq_count * seq_len, -1))
    grad_wq = matmul_left_t(a_low, d_q_low)
    grad_wk = matmul_left_t(a_low, d_k_low)
    grad_wv = matmul_left_t(a_low, d_v_low)
    d_normed_a = (
        matmul_right_t(d_q_low, q_full)
        + matmul_right_t(d_k_low, k_full)
        + matmul_right_t(d_v_low, v_full)
    )
    d_input_norm, grad_apre = pull_a(d_normed_a)
    grad_x = (d_mid + d_input_norm).astype(jnp.bfloat16)
    all_shards = (
        lax.psum_scatter(grad_wq, "fsdp", scatter_dimension=0, tiled=True),
        lax.psum_scatter(grad_wk, "fsdp", scatter_dimension=0, tiled=True),
        lax.psum_scatter(grad_wv, "fsdp", scatter_dimension=0, tiled=True),
        lax.psum_scatter(grad_wo, "fsdp", scatter_dimension=0, tiled=True),
        lax.psum_scatter(grad_apre, "fsdp", scatter_dimension=0, tiled=True),
        lax.psum_scatter(grad_apost, "fsdp", scatter_dimension=0, tiled=True),
        lax.psum_scatter(grad_qgain, "fsdp", scatter_dimension=0, tiled=True),
        lax.psum_scatter(grad_kgain, "fsdp", scatter_dimension=0, tiled=True),
        lax.psum_scatter(grad_wgate, "fsdp", scatter_dimension=0, tiled=True),
        lax.psum_scatter(grad_wup, "fsdp", scatter_dimension=0, tiled=True),
        lax.psum_scatter(grad_wdown, "fsdp", scatter_dimension=0, tiled=True),
        lax.psum_scatter(grad_mpre, "fsdp", scatter_dimension=0, tiled=True),
        lax.psum_scatter(grad_mpost, "fsdp", scatter_dimension=0, tiled=True),
    )
    all_cols = (
        lax.psum_scatter(
            all_shards[0].astype(jnp.bfloat16), "replica", scatter_dimension=1, tiled=True
        ).astype(jnp.float32),
        lax.psum_scatter(
            all_shards[1].astype(jnp.bfloat16), "replica", scatter_dimension=1, tiled=True
        ).astype(jnp.float32),
        lax.psum_scatter(
            all_shards[2].astype(jnp.bfloat16), "replica", scatter_dimension=1, tiled=True
        ).astype(jnp.float32),
        lax.psum_scatter(
            all_shards[3].astype(jnp.bfloat16), "replica", scatter_dimension=1, tiled=True
        ).astype(jnp.float32),
        lax.psum_scatter(
            all_shards[8].astype(jnp.bfloat16), "replica", scatter_dimension=1, tiled=True
        ).astype(jnp.float32),
        lax.psum_scatter(
            all_shards[9].astype(jnp.bfloat16), "replica", scatter_dimension=1, tiled=True
        ).astype(jnp.float32),
        lax.psum_scatter(
            all_shards[10].astype(jnp.bfloat16), "replica", scatter_dimension=1, tiled=True
        ).astype(jnp.float32),
        lax.psum_scatter(
            spread_gain(all_shards[4]).astype(jnp.bfloat16),
            "replica",
            scatter_dimension=1,
            tiled=True,
        ).astype(jnp.float32),
        lax.psum_scatter(
            spread_gain(all_shards[5]).astype(jnp.bfloat16),
            "replica",
            scatter_dimension=1,
            tiled=True,
        ).astype(jnp.float32),
        lax.psum_scatter(
            spread_gain(all_shards[6]).astype(jnp.bfloat16),
            "replica",
            scatter_dimension=1,
            tiled=True,
        ).astype(jnp.float32),
        lax.psum_scatter(
            spread_gain(all_shards[7]).astype(jnp.bfloat16),
            "replica",
            scatter_dimension=1,
            tiled=True,
        ).astype(jnp.float32),
        lax.psum_scatter(
            spread_gain(all_shards[11]).astype(jnp.bfloat16),
            "replica",
            scatter_dimension=1,
            tiled=True,
        ).astype(jnp.float32),
        lax.psum_scatter(
            spread_gain(all_shards[12]).astype(jnp.bfloat16),
            "replica",
            scatter_dimension=1,
            tiled=True,
        ).astype(jnp.float32),
    )
    all_mats = (
        lax.all_gather(all_cols[0].astype(jnp.bfloat16), "replica", axis=1, tiled=True).astype(
            jnp.float32
        ),
        lax.all_gather(all_cols[1].astype(jnp.bfloat16), "replica", axis=1, tiled=True).astype(
            jnp.float32
        ),
        lax.all_gather(all_cols[2].astype(jnp.bfloat16), "replica", axis=1, tiled=True).astype(
            jnp.float32
        ),
        lax.all_gather(all_cols[3].astype(jnp.bfloat16), "replica", axis=1, tiled=True).astype(
            jnp.float32
        ),
        lax.all_gather(all_cols[4].astype(jnp.bfloat16), "replica", axis=1, tiled=True).astype(
            jnp.float32
        ),
        lax.all_gather(all_cols[5].astype(jnp.bfloat16), "replica", axis=1, tiled=True).astype(
            jnp.float32
        ),
        lax.all_gather(all_cols[6].astype(jnp.bfloat16), "replica", axis=1, tiled=True).astype(
            jnp.float32
        ),
    )
    attn_sums = (
        all_mats[0],
        all_mats[1],
        all_mats[2],
        all_mats[3],
        all_cols[7][:, 0],
        all_cols[8][:, 0],
        all_cols[9][:, 0],
        all_cols[10][:, 0],
    )
    mlp_sums = (all_mats[4], all_mats[5], all_mats[6], all_cols[11][:, 0], all_cols[12][:, 0])
    return (
        layer_out,
        grad_x,
        attn_sums[0],
        attn_sums[1],
        attn_sums[2],
        attn_sums[3],
        attn_sums[4],
        attn_sums[5],
        attn_sums[6],
        attn_sums[7],
        mlp_sums[0],
        mlp_sums[1],
        mlp_sums[2],
        mlp_sums[3],
        mlp_sums[4],
    )


def solution(mesh):
    in_specs = (
        P(("replica", "fsdp"), None),
        P(("replica", "fsdp"), None),
        P(("replica", "fsdp"), None),
        P("fsdp", None),
        P("fsdp", None),
        P("fsdp", None),
        P("fsdp", None),
        P("fsdp"),
        P("fsdp"),
        P("fsdp"),
        P("fsdp"),
        P("fsdp", None),
        P("fsdp", None),
        P("fsdp", None),
        P("fsdp"),
        P("fsdp"),
    )
    out_specs = (
        P(("replica", "fsdp"), None),
        P(("replica", "fsdp"), None),
        P("fsdp", None),
        P("fsdp", None),
        P("fsdp", None),
        P("fsdp", None),
        P("fsdp"),
        P("fsdp"),
        P("fsdp"),
        P("fsdp"),
        P("fsdp", None),
        P("fsdp", None),
        P("fsdp", None),
        P("fsdp"),
        P("fsdp"),
    )
    return jax.shard_map(body, mesh=mesh, in_specs=in_specs, out_specs=out_specs, check_vma=False)
```

profile of v0, /device:TPU:10, one launch (start us, length us, event | category | flops | bytes accessed | tf_op | source)
XLA Modules:
  0.0 1966.7 jit_solution(13436216199895763823)
XLA Ops:
  20.9 53.8 %all-reduce.23 = (bf16[1152]{0:T(1024)(128)(2,1)S(1)}, bf16[256]{0:T(256)(128)(2,1)S(1)}, bf16[256]{0:T(256)(128)(2,1)S(1)}, bf16[1152]{0:T(1024)(128)(2,1)S(1)}...) all-reduce(bf16[1152]{0:T(1024)(128)(2,1)S(1)} %dynamic-update-slic, ...), channel_id=1, replica_groups=mesh['replica'=2,'fsdp'=16] {'fsdp'}, use_global_device_ids=true, to_apply=%add.4 | all-reduce | flops 5120 | bytes 20480
  78.1 24.7 %all_gather.68 = bf16[1152,256]{1,0:T(8,128)(2,1)S(1)} all-gather(bf16[72,256]{1,0:T(8,128)(2,1)S(1)} %convert_element_type.245), channel_id=1, replica_groups=mesh['replica'=2,'fsdp'=16] {'fsdp'}, dimensions={0}, use_global_device_ids=true | all-gather | bytes 626688 | tf_op jit(solution)/shard_map/all_gather | solution.py:114
  104.6 24.5 %all_gather.69 = bf16[1152,256]{1,0:T(8,128)(2,1)S(1)} all-gather(bf16[72,256]{1,0:T(8,128)(2,1)S(1)} %convert_element_type.247), channel_id=1, replica_groups=mesh['replica'=2,'fsdp'=16] {'fsdp'}, dimensions={0}, use_global_device_ids=true | all-gather | bytes 626688 | tf_op jit(solution)/shard_map/all_gather | solution.py:113
  144.9 78.7 %all-gather.12.cloned.1.call-done = bf16[1152,6912]{1,0:T(8,128)(2,1)} async-done(((bf16[72,6912]{1,0:T(8,128)(2,1)}), bf16[1152,6912]{1,0:T(8,128)(2,1)}) %all-gather.12.cloned.1.call-update) | async-done | bytes 15925264 | tf_op jit(solution)/shard_map/all_gather | solution.py:127
  223.6 13.4 fusion.97
  237.0 108.4 %all-gather.14.cloned.1.call-done = bf16[1152,6912]{1,0:T(8,128)(2,1)} async-done(((bf16[72,6912]{1,0:T(8,128)(2,1)}), bf16[1152,6912]{1,0:T(8,128)(2,1)}) %all-gather.14.cloned.1.call-update) | async-done | bytes 15925264 | tf_op jit(solution)/shard_map/all_gather | solution.py:128
  345.4 13.2 multiply_convert_fusion.1
  358.6 108.6 %all-gather.16.cloned.1.call-done = bf16[6912,1152]{1,0:T(8,128)(2,1)} async-done(((bf16[432,1152]{1,0:T(8,128)(2,1)}), bf16[6912,1152]{1,0:T(8,128)(2,1)}) %all-gather.16.cloned.1.call-update) | async-done | bytes 15925264 | tf_op jit(solution)/shard_map/all_gather | solution.py:129
  480.4 17.0 multiply_convert_fusion
  497.5 12.4 fusion.98
  509.8 13.6 multiply_reduce_fusion
  551.8 14.2 fusion.101
  566.0 13.9 fusion.102
  581.0 14.5 fusion.103
  597.3 58.9 %reduce-scatter.33.cloned.1.call-done = f32[72,256]{1,0:T(8,128)} async-done(((f32[1152,256]{1,0:T(8,128)}), f32[72,256]{1,0:T(8,128)}) %reduce-scatter.33.cloned.1.call-update) | async-done | bytes 73744 | tf_op jit(solution)/shard_map/reduce_scatter | solution.py:227
  657.9 76.2 %reduce-scatter.27.cloned.1.call-done = f32[72,1024]{1,0:T(8,128)} async-done(((f32[1152,1024]{1,0:T(8,128)}), f32[72,1024]{1,0:T(8,128)}) %reduce-scatter.27.cloned.1.call-update) | async-done | bytes 294928 | tf_op jit(solution)/shard_map/reduce_scatter | solution.py:225
  735.9 77.3 %reduce-scatter.35.cloned.1.call-done = f32[64,1152]{1,0:T(8,128)} async-done(((f32[1024,1152]{1,0:T(8,128)}), f32[64,1152]{1,0:T(8,128)}) %reduce-scatter.35.cloned.1.call-update) | async-done | bytes 294928 | tf_op jit(solution)/shard_map/reduce_scatter | solution.py:228
  815.1 320.9 %reduce-scatter.37.cloned.1.call-done = f32[72,6912]{1,0:T(8,128)} async-done(((f32[1152,6912]{1,0:T(8,128)}), f32[72,6912]{1,0:T(8,128)}) %reduce-scatter.37.cloned.1.call-update) | async-done | bytes 1990672 | tf_op jit(solution)/shard_map/reduce_scatter | solution.py:233
  1139.4 320.6 %reduce-scatter.39.cloned.1.call-done = f32[72,6912]{1,0:T(8,128)} async-done(((f32[1152,6912]{1,0:T(8,128)}), f32[72,6912]{1,0:T(8,128)}) %reduce-scatter.39.cloned.1.call-update) | async-done | bytes 1990672 | tf_op jit(solution)/shard_map/reduce_scatter | solution.py:234
  1469.4 314.4 %reduce-scatter.41.cloned.1.call-done = f32[432,1152]{1,0:T(8,128)} async-done(((f32[6912,1152]{1,0:T(8,128)}), f32[432,1152]{1,0:T(8,128)}) %reduce-scatter.41.cloned.1.call-update) | async-done | bytes 1990672 | tf_op jit(solution)/shard_map/reduce_scatter | solution.py:235
  1789.8 54.1 %all-reduce.22 = (bf16[1152]{0:T(1024)(128)(2,1)S(1)}, bf16[1152]{0:T(1024)(128)(2,1)S(1)}, bf16[256]{0:T(256)(128)(2,1)S(1)}, bf16[256]{0:T(256)(128)(2,1)S(1)}...) all-reduce(f32[1152]{0:T(1024)} %get-tuple-element.23, ...), channel_id=10, replica_groups=mesh['replica'=2,'fsdp'=16] {'fsdp'}, use_global_device_ids=true, to_apply=%region_26.27.clone | all-reduce | flops 5120 | bytes 30720
  1885.3 22.2 %all_gather.84 = bf16[72,6912]{1,0:T(8,128)(2,1)S(1)} all-gather(bf16[72,3456]{1,0:T(8,128)(2,1)S(1)} %copy.121), channel_id=1, replica_groups=mesh['replica'=2,'fsdp'=16] {'replica'}, dimensions={1}, use_global_device_ids=true | all-gather | bytes 1492992 | tf_op jit(solution)/shard_map/all_gather | solution.py:311
  1912.3 19.9 %all_gather.85 = bf16[72,6912]{1,0:T(8,128)(2,1)S(1)} all-gather(bf16[72,3456]{1,0:T(8,128)(2,1)S(1)} %copy.123), channel_id=1, replica_groups=mesh['replica'=2,'fsdp'=16] {'replica'}, dimensions={1}, use_global_device_ids=true | all-gather | bytes 1492992 | tf_op jit(solution)/shard_map/all_gather | solution.py:314
  1941.4 15.2 all-gather.1
  (352 shorter events, 157.6 us)
Async XLA Ops:
  7.2 125.7 %all-gather.8.cloned.1.call-start = ((), (), s32[]{:S(2)}) async-start(), calls=%async_computation.14 | async-start | bytes 2506752 | tf_op jit(solution)/shard_map/all_gather | solution.py:112
  8.9 130.1 %all-gather.10.cloned.1.call-start = ((), (), s32[]{:S(2)}) async-start(), calls=%async_computation.15 | async-start | bytes 2506752 | tf_op jit(solution)/shard_map/all_gather | solution.py:115
  10.6 213.0 %all-gather.12.cloned.1.call-start = ((), (), s32[]{:S(2)}) async-start(), calls=%async_computation.16 | async-start | bytes 16920576 | tf_op jit(solution)/shard_map/all_gather | solution.py:127
  13.4 331.9 %all-gather.14.cloned.1.call-start = ((), (), s32[]{:S(2)}) async-start(), calls=%async_computation.17 | async-start | bytes 16920576 | tf_op jit(solution)/shard_map/all_gather | solution.py:128
  14.7 59.9 %copy-start.40 = (f32[72,256]{1,0:T(8,128)S(1)}, f32[72,256]{1,0:T(8,128)}, u32[]{:S(2)}) copy-start(f32[72,256]{1,0:T(8,128)} %param.21) | copy-start | bytes 221188
  14.7 452.4 %all-gather.16.cloned.1.call-start = ((), (), s32[]{:S(2)}) async-start(), calls=%async_computation.18 | async-start | bytes 16920576 | tf_op jit(solution)/shard_map/all_gather | solution.py:129
  17.4 60.5 %copy-start = (bf16[256,1152]{1,0:T(8,128)(2,1)S(1)}, bf16[256,1152]{1,0:T(8,128)(2,1)}, u32[]{:S(2)}) copy-start(bf16[256,1152]{1,0:T(8,128)(2,1)} %param.16) | copy-start | bytes 1769476
  17.4 578.2 %reduce-scatter.31.cloned.1.call-start = ((), (), s32[]{:S(2)}) async-start(), calls=%async_computation.21 | async-start | bytes 1253376 | tf_op jit(solution)/shard_map/reduce_scatter | solution.py:226
  74.7 61.7 %copy-start.56 = (f32[256]{0:T(256)}, f32[256]{0:T(256)S(1)}, u32[]{:S(2)}) copy-start(f32[256]{0:T(256)S(1)} %convert_element_type.253) | copy-start | bytes 3076
  536.9 119.3 %reduce-scatter.33.cloned.1.call-start = ((), (), s32[]{:S(2)}) async-start(), calls=%async_computation.22 | async-start | bytes 1253376 | tf_op jit(solution)/shard_map/reduce_scatter | solution.py:227
  540.4 193.7 %reduce-scatter.27.cloned.1.call-start = ((), (), s32[]{:S(2)}) async-start(), calls=%async_computation.19 | async-start | bytes 5013504 | tf_op jit(solution)/shard_map/reduce_scatter | solution.py:225
  546.7 266.5 %reduce-scatter.35.cloned.1.call-start = ((), (), s32[]{:S(2)}) async-start(), calls=%async_computation.23 | async-start | bytes 5013504 | tf_op jit(solution)/shard_map/reduce_scatter | solution.py:228
  550.7 585.2 %reduce-scatter.37.cloned.1.call-start = ((), (), s32[]{:S(2)}) async-start(), calls=%async_computation.24 | async-start | bytes 33841152 | tf_op jit(solution)/shard_map/reduce_scatter | solution.py:233
  566.0 894.0 %reduce-scatter.39.cloned.1.call-start = ((), (), s32[]{:S(2)}) async-start(), calls=%async_computation.25 | async-start | bytes 33841152 | tf_op jit(solution)/shard_map/reduce_scatter | solution.py:234
  579.9 1203.9 %reduce-scatter.41.cloned.1.call-start = ((), (), s32[]{:S(2)}) async-start(), calls=%async_computation.26 | async-start | bytes 33841152 | tf_op jit(solution)/shard_map/reduce_scatter | solution.py:235
  595.5 1259.3 %reduce-scatter.43.cloned.1.call-start = ((), (), s32[]{:S(2)}) async-start(), calls=%async_computation.27 | async-start | bytes 98304
  597.2 1263.8 %reduce-scatter.45.cloned.1.call-start = ((), (), s32[]{:S(2)}) async-start(), calls=%async_computation.28 | async-start | bytes 98304
  657.9 1209.5 %reduce-scatter.29.cloned.1.call-start = ((), (), s32[]{:S(2)}) async-start(), calls=%async_computation.20 | async-start | bytes 221184 | tf_op jit(solution)/shard_map/reduce_scatter | solution.py:240
  735.8 1138.1 %reduce-scatter.47.cloned.1.call-start = ((), (), s32[]{:S(2)}) async-start(), calls=%async_computation.29 | async-start | bytes 442368
  815.1 1068.7 %reduce-scatter.49.cloned.1.call-start = ((), (), s32[]{:S(2)}) async-start(), calls=%async_computation.30 | async-start | bytes 2654208
  1139.3 771.5 %reduce-scatter.51.cloned.1.call-start = ((), (), s32[]{:S(2)}) async-start(), calls=%async_computation.31 | async-start | bytes 2654208
  1463.3 476.8 %reduce-scatter.53.cloned.1.call-start = ((), (), s32[]{:S(2)}) async-start(), calls=%async_computation.32 | async-start | bytes 1769472
  1787.2 65.9 %copy-start.63 = (f32[256]{0:T(256)S(1)}, f32[256]{0:T(256)}, u32[]{:S(2)}) copy-start(f32[256]{0:T(256)} %copy-done.62) | copy-start | bytes 3076
  1787.2 66.5 %copy-start.6 = (f32[256,1152]{1,0:T(8,128)S(1)}, f32[256,1152]{1,0:T(8,128)}, u32[]{:S(2)}) copy-start(f32[256,1152]{1,0:T(8,128)} %copy-done.5) | copy-start | bytes 3538948
  (73 other events, 444.4 us)
Sparse Core Ops, SparseCore 0:
  10.9 43.1 all-gather.7
  56.9 43.3 all-gather.9
  103.1 120.4 all-gather.11
  225.6 119.6 all-gather.13
  347.4 119.6 all-gather.15
  537.0 57.9 reduce-scatter.30
  599.2 57.0 reduce-scatter.32
  660.1 74.0 reduce-scatter.26
  738.5 74.6 reduce-scatter.34
  817.3 318.6 reduce-scatter.36
  1140.2 319.6 reduce-scatter.38
  1464.1 319.6 reduce-scatter.40
  1786.6 9.5 reduce-scatter.42
  1798.3 9.8 reduce-scatter.44
  1810.8 10.4 reduce-scatter.28
  1824.0 12.0 reduce-scatter.46
  1838.7 29.8 reduce-scatter.48
  1871.4 39.3 reduce-scatter.50
  1913.0 26.9 reduce-scatter.52
where the time goes:
time: 1970 us
  waiting for transfers between devices  1470 us (75%)
  blocking collectives  242 us (12%)
  matrix products  149 us (8%)
  other arithmetic  46.5 us (2%)
  local copies, waits for them, and re-layouts  36.5 us (2%)
    reduce_scatter x1, waiting for transfers between devices, body(): lax.psum_scatter(grad_wgate, 'fsdp', scatter_dimension=0, tiled=True)  321 us
    reduce_scatter x1, waiting for transfers between devices, body(): lax.psum_scatter(grad_wup, 'fsdp', scatter_dimension=0, tiled=True)  321 us
    reduce_scatter x1, waiting for transfers between devices, body(): lax.psum_scatter(grad_wdown, 'fsdp', scatter_dimension=0, tiled=True)  314 us
    unnamed x3, blocking collectives  113 us
    all_gather x1, waiting for transfers between devices, body(): lax.all_gather(to_low(w_down), 'fsdp', axis=0, tiled=True)  109 us
    all_gather x1, waiting for transfers between devices, body(): lax.all_gather(to_low(w_up), 'fsdp', axis=0, tiled=True)  108 us
    all_gather x1, waiting for transfers between devices, body(): lax.all_gather(to_low(w_gate), 'fsdp', axis=0, tiled=True)  78.7 us
    reduce_scatter x1, waiting for transfers between devices, body(): lax.psum_scatter(grad_wo, 'fsdp', scatter_dimension=0, tiled=True)  77.3 us
  transfers between devices with their start and end apart: 19, of which 11 were waited for; matrix products, arithmetic and copies ran while one was open for 7% of the time, Pallas kernels for 0%

commit v1 on v0

--- a/solution.py
+++ b/solution.py
@@ -4,6 +4,8 @@
 import jax
 import jax.numpy as jnp
 from jax import lax
+from jax.experimental import pallas as pl
+from jax.experimental.pallas import tpu as pltpu
 from jax.sharding import PartitionSpec as P
 
 EPS = 1e-06
@@ -90,7 +92,7 @@
     return jnp.broadcast_to(values[:, None], (values.shape[0], lax.axis_size("replica")))
 
 
-def body(
+def general_body(
     layer_in,
     d_out,
     segments,
@@ -348,6 +350,728 @@
     )
 
 
+MESH = pl.DeviceIdType.MESH
+VMEM_BYTES = 60 * 2**20
+F32 = jnp.float32
+BF16 = jnp.bfloat16
+
+
+def fits_cubes(mesh):
+    return dict(mesh.shape) == {"replica": 2, "fsdp": 16}
+
+
+class Place:
+    def __init__(self):
+        shard = lax.axis_index("fsdp")
+        self.x = lax.axis_index("replica")
+        self.shard = shard
+        self.c = lax.rem(shard, 2)
+        self.y = lax.rem(lax.div(shard, 2), 2)
+        self.z = lax.div(shard, 4)
+        self.zl = lax.rem(self.z, 2)
+        self.zh = lax.div(self.z, 2)
+
+    def at(self, x=None, y=None, z=None, c=None):
+        x = self.x if x is None else x
+        y = self.y if y is None else y
+        z = self.z if z is None else z
+        c = self.c if c is None else c
+        return (x, (z * 2 + y) * 2 + c)
+
+    def z_xor(self, k):
+        low = self.zl if k % 2 == 0 else 1 - self.zl
+        high = self.zh if k // 2 == 0 else 1 - self.zh
+        return 2 * high + low
+
+    def cube(self, bits):
+        return self.at(
+            x=1 - self.x if bits & 4 else self.x,
+            y=1 - self.y if bits & 2 else self.y,
+            z=self.z_xor(1) if bits & 1 else self.z,
+        )
+
+
+class Wires:
+    def __init__(self, send, recv):
+        self.send, self.recv, self.used = send, recv, 0
+
+    def remote(self, src, dst, device):
+        i = self.used
+        self.used += 1
+        return pltpu.make_async_remote_copy(
+            src_ref=src,
+            dst_ref=dst,
+            send_sem=self.send.at[i],
+            recv_sem=self.recv.at[i],
+            device_id=device,
+            device_id_type=MESH,
+        )
+
+    def local(self, src, dst):
+        i = self.used
+        self.used += 1
+        return pltpu.make_async_copy(src, dst, self.send.at[i])
+
+
+def greet(devices):
+    barrier = pltpu.get_barrier_semaphore()
+    for device in devices:
+        pl.semaphore_signal(barrier, inc=1, device_id=device, device_id_type=MESH)
+    pl.semaphore_wait(barrier, len(devices))
+
+
+def hbm():
+    return pl.BlockSpec(memory_space=pl.ANY)
+
+
+def vmem():
+    return pl.BlockSpec(memory_space=pltpu.VMEM)
+
+
+def sems(count):
+    return [pltpu.SemaphoreType.DMA((count,)), pltpu.SemaphoreType.DMA((count,))]
+
+
+def params(collective_id):
+    return pltpu.CompilerParams(
+        collective_id=collective_id, has_side_effects=True, vmem_limit_bytes=VMEM_BYTES
+    )
+
+
+def weights_kernel(qkv, out, gains, gu, dn, qkv_f, out_f, gains_f, gu_f, dn_f, send, recv):
+    p = Place()
+    w = Wires(send, recv)
+    x, y, z, c = p.x, p.y, p.z, p.c
+    sibling = p.at(c=1 - c)
+    plane = [p.at(x=1 - x), p.at(y=1 - y), p.at(x=1 - x, y=1 - y)]
+    lines = [p.at(y=yy, z=p.z_xor(k)) for yy in (y, 1 - y) for k in range(1, 4)]
+    greet([sibling] + plane + lines)
+
+    started, local = [], []
+
+    def push(src, dst, device):
+        copy = w.remote(src, dst, device)
+        copy.start()
+        started.append(copy)
+        return copy
+
+    def keep(src, dst):
+        copy = w.local(src, dst)
+        copy.start()
+        local.append(copy)
+        return copy
+
+    line = []
+    for k in range(1, 4):
+        to = p.at(z=p.z_xor(k))
+        line.append(
+            (
+                push(qkv.at[x], qkv_f.at[x, z, y, c], to),
+                push(out.at[x], out_f.at[z, y, c, x], to),
+                push(gains, gains_f.at[z, y, c], to),
+            )
+        )
+    own = [
+        keep(qkv, qkv_f.at[:, z, y, c]),
+        keep(out, out_f.at[z, y, c]),
+        keep(gains, gains_f.at[z, y, c]),
+    ]
+    across = [
+        [
+            push(qkv, qkv_f.at[:, z, y, c], plane[1]),
+            push(out, out_f.at[z, y, c], plane[1]),
+            push(gains, gains_f.at[z, y, c], plane[1]),
+        ]
+    ]
+    wide = []
+    for k in (3, 2, 1, 0):
+        for other in (1, 0):
+            if k == 0 and other == 0:
+                continue
+            yy = 1 - y if other else y
+            zz = p.z_xor(k)
+            part = (lax.rem(zz, 2) * 2 + x) * 2 + yy
+            copy = push(gu.at[:, part], gu_f.at[:, z, y, c], p.at(y=yy, z=zz))
+            wide.append((k, other, copy))
+    part = (p.zl * 2 + x) * 2 + y
+    own_wide = keep(gu.at[:, part], gu_f.at[:, z, y, c])
+    source_z = 2 * p.zl + x
+    down_sends = []
+    down_first = w.used
+    w.used += 3
+    for half in range(2):
+        zz = 2 * half + p.zh
+        copy = pltpu.make_async_remote_copy(
+            src_ref=dn,
+            dst_ref=dn_f.at[c],
+            send_sem=send.at[down_first + half],
+            recv_sem=recv.at[down_first],
+            device_id=p.at(z=zz),
+            device_id_type=MESH,
+        )
+        need = (x == p.zl) & (zz != z)
+        pl.when(need)(copy.start)
+        down_sends.append((need, copy))
+    own_down = pltpu.make_async_copy(dn, dn_f.at[c], send.at[down_first + 2])
+    pl.when(source_z == z)(own_down.start)
+
+    for copy in own:
+        copy.wait()
+    for k in range(1, 4):
+        zz = p.z_xor(k)
+        for copy in line[k - 1]:
+            copy.wait_recv()
+        batch = []
+        for to in plane:
+            batch.append(push(qkv_f.at[x, zz, y, c], qkv_f.at[x, zz, y, c], to))
+            batch.append(push(out_f.at[zz, y, c, x], out_f.at[zz, y, c, x], to))
+        batch.append(push(gains_f.at[zz, y, c], gains_f.at[zz, y, c], plane[1]))
+        across.append(batch)
+    pairs = []
+    for k in range(4):
+        zz = p.z_xor(k)
+        for copy in across[k]:
+            copy.wait_recv()
+        pairs.append(push(qkv_f.at[:, zz, :, c], qkv_f.at[:, zz, :, c], sibling))
+        pairs.append(push(out_f.at[zz, :, c], out_f.at[zz, :, c], sibling))
+        pairs.append(push(gains_f.at[zz, :, c], gains_f.at[zz, :, c], sibling))
+    own_wide.wait()
+    pairs.append(push(gu_f.at[:, z, y, c], gu_f.at[:, z, y, c], sibling))
+    for k, other, copy in reversed(wide):
+        copy.wait_recv()
+        zz = p.z_xor(k)
+        yy = 1 - y if other else y
+        pairs.append(push(gu_f.at[:, zz, yy, c], gu_f.at[:, zz, yy, c], sibling))
+    pl.when(source_z == z)(own_down.wait)
+    pl.when(source_z != z)(down_sends[0][1].wait_recv)
+    pairs.append(push(dn_f.at[c], dn_f.at[c], sibling))
+    for copy in pairs:
+        copy.wait_recv()
+    for need, copy in down_sends:
+        pl.when(need)(copy.wait_send)
+    for copy in started:
+        copy.wait_send()
+
+
+def gather_weights(qkv, out, gains, gu, dn):
+    _, rows, columns = qkv.shape
+    _, out_rows, out_columns = out.shape
+    shapes = (
+        jax.ShapeDtypeStruct((2, 4, 2, 2, rows, columns), BF16),
+        jax.ShapeDtypeStruct((4, 2, 2, 2, out_rows, out_columns), BF16),
+        jax.ShapeDtypeStruct((4, 2, 2) + gains.shape, F32),
+        jax.ShapeDtypeStruct((2, 4, 2, 2) + gu.shape[2:], BF16),
+        jax.ShapeDtypeStruct((2,) + dn.shape, BF16),
+    )
+    return pl.pallas_call(
+        weights_kernel,
+        out_shape=shapes,
+        in_specs=[hbm()] * 5,
+        out_specs=(hbm(),) * 5,
+        scratch_shapes=sems(96),
+        compiler_params=params(0),
+        name="gather_weights",
+    )(qkv, out, gains, gu, dn)
+
+
+X, Y, Z = 4, 2, 1
+
+
+def thirds(rows):
+    first = -(-rows // 48) * 16
+    return ((0, first), (first, first), (2 * first, rows - 2 * first))
+
+
+def cube_gather_kernel(block, every, send, recv):
+    p = Place()
+    w = Wires(send, recv)
+    near = {bit: p.cube(bit) for bit in (X, Y, Z)}
+    greet([near[X], near[Y], near[Z]])
+    started = []
+
+    def push(src, dst, bit):
+        copy = w.remote(src, dst, near[bit])
+        copy.start()
+        started.append(copy)
+        return copy
+
+    rows = block.shape[0]
+    half = rows // 2
+    own = w.local(block, every.at[0])
+    own.start()
+    arrivals = {}
+    for h in range(2):
+        at = pl.ds(h * half, half)
+        for bit in (X, Y, Z):
+            arrivals[bit, h] = push(block.at[at], every.at[bit, at], bit)
+    for h in range(2):
+        at = pl.ds(h * half, half)
+        for link, relay in ((X, Y), (Y, Z), (Z, X)):
+            arrivals[relay, h].wait_recv()
+            arrivals[link | relay, h] = push(every.at[relay, at], every.at[link | relay, at], link)
+    last = []
+    for h in range(2):
+        for (start, size), link, relay in zip(thirds(half), (X, Y, Z), (Y | Z, X | Z, X | Y)):
+            at = pl.ds(h * half + start, size)
+            arrivals[relay, h].wait_recv()
+            last.append(push(every.at[relay, at], every.at[7, at], link))
+    for copy in last:
+        copy.wait_recv()
+    own.wait()
+    for copy in started:
+        copy.wait_send()
+
+
+def cube_gather(block):
+    return pl.pallas_call(
+        cube_gather_kernel,
+        out_shape=jax.ShapeDtypeStruct((8,) + block.shape, block.dtype),
+        in_specs=[hbm()],
+        out_specs=hbm(),
+        scratch_shapes=sems(24),
+        compiler_params=params(1),
+        name="cube_gather",
+    )(block)
+
+
+def cube_sum_kernel(parts, total, ready, third, second, first, send, recv):
+    p = Place()
+    w = Wires(send, recv)
+    near = {bit: p.cube(bit) for bit in (X, Y, Z)}
+    greet([near[X], near[Y], near[Z]])
+    started = []
+
+    def push(src, dst, bit):
+        copy = w.remote(src, dst, near[bit])
+        copy.start()
+        started.append(copy)
+        return copy
+
+    rows = total.shape[0]
+    half = rows // 2
+    far, mid, end = {}, {}, {}
+    for h in range(2):
+        for (start, size), link in zip(thirds(half), (X, Y, Z)):
+            at = pl.ds(h * half + start, size)
+            far[link, h] = push(parts.at[7, at], third.at[at], link)
+    for h in range(2):
+        for i, (link, onward, place) in enumerate(((X, Y, Y | Z), (Y, Z, X | Z), (Z, X, X | Y))):
+            start, size = thirds(half)[i]
+            at = pl.ds(h * half + start, size)
+            all_at = pl.ds(h * half, half)
+            far[link, h].wait_recv()
+            ready[i, all_at] = parts[place, all_at]
+            ready[i, at] = (parts[place, at].astype(F32) + third[at].astype(F32)).astype(BF16)
+            mid[onward, h] = push(ready.at[i, all_at], second.at[i, all_at], onward)
+    for h in range(2):
+        at = pl.ds(h * half, half)
+        for i, (came, place) in enumerate(((Y, Z), (Z, X), (X, Y))):
+            mid[came, h].wait_recv()
+            ready[3 + i, at] = (parts[place, at].astype(F32) + second[i, at].astype(F32)).astype(BF16)
+            end[place, h] = push(ready.at[3 + i, at], first.at[i, at], place)
+    for h in range(2):
+        at = pl.ds(h * half, half)
+        value = parts[0, at].astype(F32)
+        for i, place in enumerate((Z, X, Y)):
+            end[place, h].wait_recv()
+            value = value + first[i, at].astype(F32)
+        total[at, :] = value
+    for copy in started:
+        copy.wait_send()
+
+
+def cube_sum(parts):
+    _, rows, columns = parts.shape
+    return pl.pallas_call(
+        cube_sum_kernel,
+        out_shape=jax.ShapeDtypeStruct((rows, columns), F32),
+        in_specs=[vmem()],
+        out_specs=vmem(),
+        scratch_shapes=[
+            pltpu.VMEM((6, rows, columns), BF16),
+            pltpu.VMEM((rows, columns), BF16),
+            pltpu.VMEM((3, rows, columns), BF16),
+            pltpu.VMEM((3, rows, columns), BF16),
+        ]
+        + sems(24),
+        compiler_params=params(2),
+        name="cube_sum",
+    )(parts)
+
+
+def add(left, right):
+    return (left.astype(F32) + right.astype(F32)).astype(BF16)
+
+
+def mlp_grads_kernel(gu, dn, gu_out, dn_out, sum1, got1, dsum1, dgot1, got2, dgot2, sum2, dsum2, send, recv):
+    p = Place()
+    w = Wires(send, recv)
+    x, y, z, c, zl, zh = p.x, p.y, p.z, p.c, p.zl, p.zh
+    sibling = p.at(c=1 - c)
+    partner = p.at(z=p.z_xor(2))
+    cube = [p.cube(bits) for bits in range(1, 8)]
+    greet([sibling, partner] + cube)
+    one = w.remote(gu.at[:, :, :, 1 - c], got1, sibling)
+    one.start()
+    two = w.remote(dn.at[1 - c], dgot1, sibling)
+    two.start()
+    one.wait_recv()
+    for part in range(2):
+        for zz in range(2):
+            for yy in range(2):
+                at = 2 * (1 - zh) + zz
+                sum1[part, 0, zz, yy] = add(gu[part, at, yy, c], got1[part, at, yy])
+    over = w.remote(sum1.at[:, 0], got2, partner)
+    over.start()
+    two.wait_recv()
+    dsum1[...] = add(dn[c], dgot1[...])
+    down_over = w.remote(dsum1, dgot2, partner)
+    mine = zl == zh
+    pl.when(zl != zh)(down_over.start)
+    for part in range(2):
+        for zz in range(2):
+            for yy in range(2):
+                at = 2 * zh + zz
+                sum1[part, 1, zz, yy] = add(gu[part, at, yy, c], got1[part, at, yy])
+    over.wait_recv()
+    sum2[...] = add(sum1[:, 1], got2[...])
+    part = (zl * 2 + x) * 2 + y
+    spread = []
+    for bits in range(1, 8):
+        zz = 1 - zl if bits & 1 else zl
+        yy = 1 - y if bits & 2 else y
+        copy = w.remote(sum2.at[:, zz, yy], gu_out.at[:, part], cube[bits - 1])
+        copy.start()
+        spread.append(copy)
+    own = w.local(sum2.at[:, zl, y], gu_out.at[:, part])
+    own.start()
+
+    away = [mine & ((x != xx) | (zh != x)) for xx in range(2)]
+    arrival = pltpu.make_async_remote_copy(
+        src_ref=dsum2,
+        dst_ref=dn_out,
+        send_sem=send.at[w.used],
+        recv_sem=recv.at[w.used],
+        device_id=sibling,
+        device_id_type=MESH,
+    )
+    arrive_sem = recv.at[w.used]
+    w.used += 1
+    down = [
+        pltpu.make_async_remote_copy(
+            src_ref=dsum2,
+            dst_ref=dn_out,
+            send_sem=send.at[w.used + xx],
+            recv_sem=arrive_sem,
+            device_id=p.at(x=xx, z=2 * zh + x),
+            device_id_type=MESH,
+        )
+        for xx in range(2)
+    ]
+    w.used += 2
+    own_down = w.local(dsum2, dn_out)
+    self_down = mine & (x == zl)
+
+    @pl.when(mine)
+    def _():
+        down_over.wait_recv()
+        dsum2[...] = add(dsum1[...], dgot2[...])
+
+    for need, copy in zip(away, down):
+        pl.when(need)(copy.start)
+    pl.when(self_down)(own_down.start)
+    pl.when(self_down)(own_down.wait)
+    pl.when(jnp.logical_not(self_down))(arrival.wait_recv)
+    for need, copy in zip(away, down):
+        pl.when(need)(copy.wait_send)
+    own.wait()
+    for copy in spread:
+        copy.wait_recv()
+    for copy in [one, two, over] + spread:
+        copy.wait_send()
+    pl.when(zl != zh)(down_over.wait_send)
+
+
+def mlp_grads(gu, dn):
+    rows, columns = gu.shape[-2:]
+    down = dn.shape[1:]
+    return pl.pallas_call(
+        mlp_grads_kernel,
+        out_shape=(
+            jax.ShapeDtypeStruct((2, 8, rows, columns), BF16),
+            jax.ShapeDtypeStruct(down, BF16),
+        ),
+        in_specs=[vmem(), vmem()],
+        out_specs=(vmem(), vmem()),
+        scratch_shapes=[
+            pltpu.VMEM((2, 2, 2, 2, rows, columns), BF16),
+            pltpu.VMEM((2, 4, 2, rows, columns), BF16),
+            pltpu.VMEM(down, BF16),
+            pltpu.VMEM(down, BF16),
+            pltpu.VMEM((2, 2, 2, rows, columns), BF16),
+            pltpu.VMEM(down, BF16),
+            pltpu.VMEM((2, 2, 2, rows, columns), BF16),
+            pltpu.VMEM(down, BF16),
+        ]
+        + sems(24),
+        compiler_params=params(3),
+        name="mlp_grads",
+    )(gu, dn)
+
+
+def attn_grads_kernel(
+    qkv, out, gains, qkv_r, out_r, gains_r,
+    q1, o1, g1, qs, os, gs, q2, o2, g2, qt, ot, gt, q3, o3, g3, send, recv,
+):
+    p = Place()
+    w = Wires(send, recv)
+    x, y, z, c = p.x, p.y, p.z, p.c
+    sibling = p.at(c=1 - c)
+    line = [p.at(z=p.z_xor(k)) for k in range(1, 4)]
+    plane = [p.at(x=1 - x), p.at(y=1 - y), p.at(x=1 - x, y=1 - y)]
+    greet([sibling] + line + plane)
+    started = []
+
+    def push(src, dst, device):
+        copy = w.remote(src, dst, device)
+        copy.start()
+        started.append(copy)
+        return copy
+
+    first = [
+        push(qkv.at[:, :, :, 1 - c], q1, sibling),
+        push(out.at[:, :, 1 - c], o1, sibling),
+        push(gains.at[:, :, 1 - c], g1, sibling),
+    ]
+    for copy in first:
+        copy.wait_recv()
+    second = []
+    for i in (2, 0, 1):
+        xx = x if i == 1 else 1 - x
+        yy = y if i == 0 else 1 - y
+        qs[i] = add(qkv[xx, :, yy, c], q1[xx, :, yy])
+        os[i] = add(out[:, yy, c, xx], o1[:, yy, xx])
+        gs[i] = gains[:, yy, c] + g1[:, yy]
+        second += [
+            push(qs.at[i], q2.at[i], plane[i]),
+            push(os.at[i], o2.at[i], plane[i]),
+            push(gs.at[i], g2.at[i], plane[i]),
+        ]
+    for copy in second:
+        copy.wait_recv()
+    qt[...] = add(
+        qkv[x, :, y, c].astype(F32) + q1[x, :, y].astype(F32) + q2[0].astype(F32),
+        q2[1].astype(F32) + q2[2].astype(F32),
+    )
+    ot[...] = add(
+        out[:, y, c, x].astype(F32) + o1[:, y, x].astype(F32) + o2[0].astype(F32),
+        o2[1].astype(F32) + o2[2].astype(F32),
+    )
+    gt[...] = gains[:, y, c] + g1[:, y] + g2[0] + g2[1] + g2[2]
+    third = []
+    for k in range(1, 4):
+        zz = p.z_xor(k)
+        third += [
+            push(qt.at[zz], q3.at[k - 1], line[k - 1]),
+            push(ot.at[zz], o3.at[k - 1], line[k - 1]),
+            push(gt.at[zz], g3.at[k - 1], line[k - 1]),
+        ]
+    for copy in third:
+        copy.wait_recv()
+    qkv_r[x] = add(qt[z].astype(F32) + q3[0].astype(F32), q3[1].astype(F32) + q3[2].astype(F32))
+    out_r[x] = add(ot[z].astype(F32) + o3[0].astype(F32), o3[1].astype(F32) + o3[2].astype(F32))
+    gains_r[...] = gt[z] + g3[0] + g3[1] + g3[2]
+    last = [
+        push(qkv_r.at[x], qkv_r.at[x], plane[0]),
+        push(out_r.at[x], out_r.at[x], plane[0]),
+    ]
+    for copy in last:
+        copy.wait_recv()
+    for copy in started:
+        copy.wait_send()
+
+
+def attn_grads(qkv, out, gains):
+    rows, columns = qkv.shape[-2:]
+    out_rows, out_columns = out.shape[-2:]
+    gain = gains.shape[-2:]
+    q, o = (rows, columns), (out_rows, out_columns)
+    scratch = []
+    for lead_q, lead_o, lead_g in (
+        ((2, 4, 2), (4, 2, 2), (4, 2)),
+        ((3, 4), (3, 4), (3, 4)),
+        ((3, 4), (3, 4), (3, 4)),
+        ((4,), (4,), (4,)),
+        ((3,), (3,), (3,)),
+    ):
+        scratch += [
+            pltpu.VMEM(lead_q + q, BF16),
+            pltpu.VMEM(lead_o + o, BF16),
+            pltpu.VMEM(lead_g + gain, F32),
+        ]
+    return pl.pallas_call(
+        attn_grads_kernel,
+        out_shape=(
+            jax.ShapeDtypeStruct((2,) + q, BF16),
+            jax.ShapeDtypeStruct((2,) + o, BF16),
+            jax.ShapeDtypeStruct(gain, F32),
+        ),
+        in_specs=[vmem()] * 3,
+        out_specs=(vmem(),) * 3,
+        scratch_shapes=scratch + sems(32),
+        compiler_params=params(4),
+        name="attn_grads",
+    )(qkv, out, gains)
+
+
+def pack_gains(vectors):
+    lead = vectors[0].shape[:-1]
+    rows = [jnp.pad(v, [(0, 0)] * len(lead) + [(0, 128 - v.shape[-1])]) for v in vectors]
+    rows += [jnp.zeros(lead + (128,), F32)] * (8 - len(rows))
+    return jnp.stack(rows, axis=-2)
+
+
+def unpack_gains(packed, sizes):
+    lead = packed.shape[:-2]
+    return [packed[..., i, :size] for i, size in enumerate(sizes)]
+
+
+def cube_body(
+    layer_in, d_out, segments, w_q, w_k, w_v, w_o, attn_pre, attn_post, q_gain, k_gain,
+    w_gate, w_up, w_down, mlp_pre, mlp_post,
+):
+    width = layer_in.shape[1]
+    head = q_gain.shape[0] * 16
+    mix = w_o.shape[0] * 16
+    hidden_units = w_gate.shape[1]
+    rows = w_q.shape[0]
+    qkv = to_low(jnp.concatenate([w_q, w_k, w_v], axis=1))
+    half = qkv.shape[1] // 2
+    qkv = jnp.stack([qkv[:, :half], qkv[:, half:]])
+    out = to_low(w_o).reshape(2, -1, width)
+    gain_list = [attn_pre, attn_post, mlp_pre, mlp_post, q_gain, k_gain]
+    gain_sizes = [v.shape[0] for v in gain_list]
+    gains = pack_gains([to_low(v).astype(F32) for v in gain_list])
+    gu = jnp.stack(
+        [to_low(w).reshape(rows, 8, -1).transpose(1, 0, 2) for w in (w_gate, w_up)]
+    )
+    qkv_f, out_f, gains_f, gu_f, dn_f = gather_weights(qkv, out, gains, gu, to_low(w_down))
+    qkv_f = qkv_f.reshape(2, width, half)
+    o_full = out_f.reshape(mix, width)
+    gain_apre, gain_apost, gain_mpre, gain_mpost, gain_q, gain_k = [
+        v.reshape(-1) for v in unpack_gains(gains_f, gain_sizes)
+    ]
+    gate_w, up_w = gu_f[0].reshape(width, -1), gu_f[1].reshape(width, -1)
+    down_w = dn_f.reshape(-1, width)
+
+    seq_count, seq_len = segments.shape
+    tok_flat = layer_in.astype(F32)
+    cosine, sine = angle_tables(segments, head)
+    masks = attention_masks(segments)
+    normed_a, pull_a = jax.vjp(norm_rows, tok_flat, gain_apre)
+    a_low = to_low(normed_a)
+    qkv_proj = jnp.concatenate([matmul(a_low, qkv_f[0]), matmul(a_low, qkv_f[1])], axis=1)
+    q_proj = qkv_proj[:, :mix].reshape(seq_count, seq_len, -1)
+    k_proj = qkv_proj[:, mix : mix + head].reshape(seq_count, seq_len, -1)
+    v_proj = qkv_proj[:, mix + head :]
+    q_rot, pull_q = jax.vjp(partial(query_path, cosine=cosine, sine=sine), q_proj, gain_q)
+    k_rot, pull_k = jax.vjp(partial(key_path, cosine=cosine, sine=sine), k_proj, gain_k)
+    q_low = to_low(q_rot)
+    k_low = to_low(k_rot)
+    v_low = to_low(v_proj).reshape(seq_count, seq_len, -1)
+    scores = scores_of(q_low, k_low, masks)
+    top_val = jnp.max(scores, axis=-1, keepdims=True)
+    expo = jnp.exp(scores - top_val)
+    probs = expo / jnp.sum(expo, axis=-1, keepdims=True)
+    p_low = to_low(probs)
+    attn_mix = jnp.einsum("nhqk,nkd->nqhd", p_low, v_low, preferred_element_type=F32)
+    o_low = to_low(attn_mix.reshape(seq_count * seq_len, -1))
+    attn_proj = matmul(o_low, o_full)
+    post_attn, pull_pa = jax.vjp(norm_rows, attn_proj, gain_apost)
+    h_mid = tok_flat + post_attn
+    normed_m, pull_m = jax.vjp(norm_rows, h_mid, gain_mpre)
+    m_all = cube_gather(to_low(normed_m)).reshape(-1, width)
+    gate_val = matmul(m_all, gate_w)
+    up_val = matmul(m_all, up_w)
+    hidden, pull_h = jax.vjp(gelu_product, gate_val, up_val)
+    h_low = to_low(hidden)
+    down_val = cube_sum(to_low(matmul(h_low, down_w)).reshape(8, -1, width))
+    post_mlp, pull_pm = jax.vjp(norm_rows, down_val, gain_mpost)
+    layer_out = (h_mid + post_mlp).astype(BF16)
+
+    grad_top = d_out.astype(F32)
+    d_down, grad_mpost = pull_pm(grad_top)
+    dd_all = cube_gather(to_low(d_down)).reshape(-1, width)
+    grad_wdown = matmul_left_t(h_low, dd_all)
+    d_hidden = matmul_right_t(dd_all, down_w)
+    d_gate, d_up = pull_h(d_hidden)
+    d_gate_low = to_low(d_gate)
+    d_up_low = to_low(d_up)
+    grad_gu = jnp.stack(
+        [to_low(matmul_left_t(m_all, d_gate_low)), to_low(matmul_left_t(m_all, d_up_low))]
+    )
+    d_normed = cube_sum(
+        to_low(matmul_right_t(d_gate_low, gate_w) + matmul_right_t(d_up_low, up_w)).reshape(
+            8, -1, width
+        )
+    )
+    gu_r, dn_r = mlp_grads(
+        grad_gu.reshape(2, 4, 2, 2, rows, -1), to_low(grad_wdown).reshape(2, -1, width)
+    )
+    d_mid_norm, grad_mpre = pull_m(d_normed)
+    d_mid = grad_top + d_mid_norm
+    d_attn, grad_apost = pull_pa(d_mid)
+    d_attn_low = to_low(d_attn)
+    grad_wo = matmul_left_t(o_low, d_attn_low)
+    d_mix_low = to_low(matmul_right_t(d_attn_low, o_full)).reshape(seq_count, seq_len, -1, head)
+    d_probs = jnp.einsum("nqhd,nkd->nhqk", d_mix_low, v_low, preferred_element_type=F32)
+    row_dot = jnp.sum(probs * d_probs, axis=-1, keepdims=True)
+    d_scores_low = to_low(probs * (d_probs - row_dot))
+    d_query = SCALE * jnp.einsum("nhqk,nkd->nqhd", d_scores_low, k_low, preferred_element_type=F32)
+    d_key = SCALE * jnp.einsum("nhqk,nqhd->nkd", d_scores_low, q_low, preferred_element_type=F32)
+    d_value = jnp.einsum("nhqk,nqhd->nkd", p_low, d_mix_low, preferred_element_type=F32)
+    d_qproj, grad_qgain = pull_q(d_query)
+    d_kproj, grad_kgain = pull_k(d_key)
+    d_qkv = to_low(
+        jnp.concatenate(
+            [v.reshape(seq_count * seq_len, -1) for v in (d_qproj, d_kproj, d_value)], axis=1
+        )
+    )
+    grad_qkv = jnp.stack(
+        [to_low(matmul_left_t(a_low, d_qkv[:, :half])), to_low(matmul_left_t(a_low, d_qkv[:, half:]))]
+    )
+    d_normed_a = matmul_right_t(d_qkv[:, :half], qkv_f[0]) + matmul_right_t(d_qkv[:, half:], qkv_f[1])
+    d_input_norm, grad_apre = pull_a(d_normed_a)
+    grad_x = (d_mid + d_input_norm).astype(BF16)
+    grad_gains = [grad_apre, grad_apost, grad_mpre, grad_mpost, grad_qgain, grad_kgain]
+    packed = pack_gains([v.reshape(4, 2, 2, -1) for v in grad_gains])
+    qkv_r, out_r, gains_r = attn_grads(
+        grad_qkv.reshape(2, 4, 2, 2, rows, half),
+        to_low(grad_wo).reshape(4, 2, 2, 2, -1, width),
+        packed,
+    )
+    qkv_r = jnp.concatenate([qkv_r[0], qkv_r[1]], axis=1).astype(F32)
+    g_apre, g_apost, g_mpre, g_mpost, g_q, g_k = unpack_gains(gains_r, gain_sizes)
+    gu_r = gu_r.transpose(0, 2, 1, 3).reshape(2, rows, hidden_units).astype(F32)
+    return (
+        layer_out,
+        grad_x,
+        qkv_r[:, :mix],
+        qkv_r[:, mix : mix + head],
+        qkv_r[:, mix + head :],
+        out_r.reshape(-1, width).astype(F32),
+        g_apre,
+        g_apost,
+        g_q,
+        g_k,
+        gu_r[0],
+        gu_r[1],
+        dn_r.astype(F32),
+        g_mpre,
+        g_mpost,
+    )
+
+
 def solution(mesh):
     in_specs = (
         P(("replica", "fsdp"), None),
@@ -384,4 +1108,5 @@
         P("fsdp"),
         P("fsdp"),
     )
+    body = cube_body if fits_cubes(mesh) else general_body
     return jax.shard_map(body, mesh=mesh, in_specs=in_specs, out_specs=out_specs, check_vma=False)

time: 1970 us -> 637 us (0.32)
  waiting for transfers between devices: 1470 us -> 0 us
  Pallas kernels: 0 us -> 431 us
  blocking collectives: 242 us -> 0 us
  matrix products: 149 us -> 92.7 us
    reduce_scatter x8 -> x0, waiting for transfers between devices: 1170 us -> none  [the longest x1 321 us: body(): lax.psum_scatter(grad_wgate, 'fsdp', scatter_dimension=0, tiled=True)]
    pallas_call x0 -> x7, Pallas kernels: none -> 431 us  [the longest x1 120 us: mlp_grads(): pl.pallas_call(mlp_grads_kernel, out_shape=(jax.ShapeDtypeStruct((2, 8, r...]
    all_gather x5 -> x0, waiting for transfers between devices: 296 us -> none  [the longest x1 109 us: body(): lax.all_gather(to_low(w_down), 'fsdp', axis=0, tiled=True)]
    all_gather x9 -> x0, blocking collectives: 130 us -> none  [the longest x1 24.7 us: body(): lax.all_gather(to_low(w_v), 'fsdp', axis=0, tiled=True)]
    unnamed x3 -> x0, blocking collectives: 113 us -> none
    dot_general x7 -> x6, matrix products: 51.5 us -> 29.7 us  [matmul_left_t(): lax.dot_general(left, right, (((0,), (0,)), ((), ())), preferred_element_...]
    unnamed x188 -> x176, local copies, waits for them, and re-layouts: 30.6 us -> 9.57 us
    dot_general x7 -> x6, matrix products: 43.7 us -> 24.1 us  [matmul(): return jnp.dot(left, right, preferred_element_type=jnp.float32)]
  transfers between devices with their start and end apart: 19 -> 0, of which waited for: 11 -> 0; matrix products, arithmetic and copies ran while one was open for 7% -> 0% of each run, Pallas kernels for 0% -> 0%
where the time goes in v1:
time: 637 us; the launch traced here: 628 us
  Pallas kernels  431 us (68%)
  matrix products  92.7 us (15%)
  local copies, waits for them, and re-layouts  53.6 us (8%)
  other arithmetic  47 us (7%)
    pallas_call x1, Pallas kernels, mlp_grads(): pl.pallas_call(mlp_grads_kernel, out_shape=(jax.ShapeDtypeStruct((2, 8, r...  120 us
    pallas_call x1, Pallas kernels, gather_weights(): pl.pallas_call(weights_kernel, out_shape=shapes, in_specs=[hbm()] * 5, ou...  91.8 us
    pallas_call x2, Pallas kernels, cube_sum(): pl.pallas_call(cube_sum_kernel, out_shape=jax.ShapeDtypeStruct((rows, col...  74.4 us
    pallas_call x2, Pallas kernels, cube_gather(): pl.pallas_call(cube_gather_kernel, out_shape=jax.ShapeDtypeStruct((8,) +...  73.6 us
    pallas_call x1, Pallas kernels, attn_grads(): pl.pallas_call(attn_grads_kernel, out_shape=(jax.ShapeDtypeStruct((2,) +...  70.9 us
    dot_general x6, matrix products, matmul_right_t(): lax.dot_general(left, right, (((1,), (1,)), ((), ())), preferred_element_...  34 us
    dot_general x6, matrix products, matmul_left_t(): lax.dot_general(left, right, (((0,), (0,)), ((), ())), preferred_element_...  29.7 us
    dot_general x6, matrix products, matmul(): return jnp.dot(left, right, preferred_element_type=jnp.float32)  24.1 us

profile of v1, /device:TPU:10, one launch (start us, length us, event | category | flops | bytes accessed | tf_op | source)
XLA Modules:
  0.0 627.5 jit_solution(7196049677622432453)
XLA Ops:
  16.7 91.8 %gather_weights.1 = (bf16[2,4,2,2,72,768]{5,4,3,2,1,0:T(8,128)(2,1)}, bf16[4,2,2,2,32,1152]{5,4,3,2,1,0:T(8,128)(2,1)}, f32[4,2,2,8,128]{4,3,2,1,0:T(8,128)}, bf...) custom-call(bf16[2,72,768]{2,1,0:T(8,128)(2,1)} %pad_maximum_fusion.9.qkv, bf16[2,32,1152]{2,1,0:T(8,128)(2,1)} %bitcast.233, ...), custom_call_target="tpu_custom_call" | custom-call | tf_op jit(solution)/shard_map/gather_weights/pallas_call | solution.py:566
  130.6 41.2 %cube_gather.2 = bf16[8,256,1152]{2,1,0:T(8,128)(2,1)} custom-call(bf16[256,1152]{1,0:T(8,128)(2,1)} %multiply_convert_fusion.2.block), custom_call_target="tpu_custom_call" | custom-call | tf_op jit(solution)/shard_map/cube_gather/pallas_call | solution.py:626
  175.4 5.2 fusion.88
  180.6 8.6 %multiply_convert_fusion.1 = (bf16[2048,864]{0,1:T(8,128)(2,1)S(1)}, f32[2048,864]{0,1:T(8,128)}) fusion(f32[2048,864]{0,1:T(8,128)S(1)} %fusion.88, bf16[2048,1152]{1,0:T(8,128)(2,1)S(1)} %bitcast.217, bf16[1152,864]{1,0:T(8,128)(2,1)S(1)} %bitcast.227), kind=kOutput, calls=%fused_computation.12 | convolution fusion | flops 4094558208 | bytes 24403968 | tf_op jit(solution)/shard_map/dot_general | solution.py:64
  189.2 7.7 %convolution_convert_fusion = bf16[2048,1152]{1,0:T(8,128)(2,1)} fusion(bf16[2048,864]{0,1:T(8,128)(2,1)S(1)} %get-tuple-element.92, bf16[864,1152]{1,0:T(8,128)(2,1)S(1)} %bitcast.246), kind=kOutput, calls=%fused_computation.3 | convolution fusion | flops 4079222784 | bytes 10248192 | tf_op jit(solution)/shard_map/dot_general | solution.py:64
  196.9 36.3 %cube_sum.2 = f32[256,1152]{1,0:T(8,128)} custom-call(bf16[8,256,1152]{2,1,0:T(8,128)(2,1)} %bitcast.214), custom_call_target="tpu_custom_call" | custom-call | tf_op jit(solution)/shard_map/cube_sum/pallas_call | solution.py:685
  238.9 32.3 %cube_gather.3 = bf16[8,256,1152]{2,1,0:T(8,128)(2,1)} custom-call(bf16[256,1152]{1,0:T(8,128)(2,1)} %get-tuple-element.68.block), custom_call_target="tpu_custom_call" | custom-call | tf_op jit(solution)/shard_map/cube_gather/pallas_call | solution.py:626
  271.3 9.6 %convolution_convert_fusion.4 = bf16[864,1152]{1,0:T(8,128)(2,1)} fusion(bf16[2048,864]{0,1:T(8,128)(2,1)} %copy-done.83, bf16[2048,1152]{1,0:T(8,128)(2,1)} %bitcast.221), kind=kOutput, calls=%fused_computation.20 | convolution fusion | flops 4077858816 | bytes 10248192 | tf_op jit(solution)/shard_map/dot_general | solution.py:68
  280.9 12.8 %multiply_convert_fusion = (bf16[2048,864]{0,1:T(8,128)(2,1)}, bf16[2048,864]{0,1:T(8,128)(2,1)S(1)}) fusion(f32[2048,864]{0,1:T(8,128)} %copy-done.82, f32[2048,864]{0,1:T(8,128)} %get-tuple-element.93, bf16[2048,1152]{1,0:T(8,128)(2,1)S(1)} %bitcast.222, bf16[864,1152]{1,0:T(8,128)(2,1)S(1)} %bitcast.247), kind=kOutput, calls=%fused_computation.11 | convolution fusion | flops 4119330816 | bytes 27942912 | tf_op jit(solution)/shard_map/dot_general | solution.py:74
  295.5 5.9 convolution_convert_fusion.3
  301.4 4.2 copy.139
  305.6 9.4 %convolution_convert_fusion.2 = bf16[1152,864]{0,1:T(8,128)(2,1)} fusion(bf16[2048,864]{0,1:T(8,128)(2,1)} %get-tuple-element.56, bf16[2048,1152]{1,0:T(8,128)(2,1)} %bitcast.215), kind=kOutput, calls=%fused_computation.18 | convolution fusion | flops 4077858816 | bytes 10248192 | tf_op jit(solution)/shard_map/dot_general | solution.py:68
  315.0 4.1 copy.140
  319.1 4.7 pad_maximum_fusion.gu
  323.8 120.4 %mlp_grads.1 = (bf16[2,8,72,864]{3,2,1,0:T(8,128)(2,1)}, bf16[432,1152]{1,0:T(8,128)(2,1)}) custom-call(bf16[2,4,2,2,72,864]{5,4,3,2,1,0:T(8,128)(2,1)} %pad_maximum_fusion.gu, bf16[2,432,1152]{2,1,0:T(8,128)(2,1)} %bitcast.231), custom_call_target="tpu_custom_call" | custom-call | tf_op jit(solution)/shard_map/mlp_grads/pallas_call | solution.py:798
  449.3 3.1 squeeze.46
  452.4 3.3 copy.142
  455.7 2.9 squeeze.47
  458.6 2.8 convert_element_type.216
  461.3 7.8 %fusion.89 = f32[2048,1152]{1,0:T(8,128)S(1)} fusion(bf16[2048,864]{0,1:T(8,128)(2,1)} %copy-done.84, bf16[1152,864]{1,0:T(8,128)(2,1)S(1)} %bitcast.230), kind=kOutput, calls=%fused_computation.204 | convolution fusion | flops 4076863488 | bytes 14966784 | tf_op jit(solution)/shard_map/dot_general | solution.py:74
  469.1 7.5 %add_convert_fusion = bf16[2048,1152]{1,0:T(8,128)(2,1)} fusion(f32[2048,1152]{1,0:T(8,128)S(1)} %fusion.89, bf16[2048,864]{0,1:T(8,128)(2,1)S(1)} %copy-done.85, bf16[1152,864]{1,0:T(8,128)(2,1)S(1)} %bitcast.228), kind=kOutput, calls=%fused_computation.2 | convolution fusion | flops 4081582080 | bytes 19685376 | tf_op jit(solution)/shard_map/dot_general | solution.py:74
  476.6 38.1 %cube_sum.3 = f32[256,1152]{1,0:T(8,128)} custom-call(bf16[8,256,1152]{2,1,0:T(8,128)(2,1)} %bitcast.213), custom_call_target="tpu_custom_call" | custom-call | tf_op jit(solution)/shard_map/cube_sum/pallas_call | solution.py:685
  542.6 3.3 convolution_convert_fusion.1
  549.7 70.9 %attn_grads.1 = (bf16[2,72,768]{2,1,0:T(8,128)(2,1)}, bf16[2,32,1152]{2,1,0:T(8,128)(2,1)}, f32[8,128]{1,0:T(8,128)}) custom-call(bf16[2,4,2,2,72,768]{5,4,3,2,1,0:T(8,128)(2,1)} %pad_maximum_fusion.1.qkv, bf16[4,2,2,2,32,1152]{5,4,3,2,1,0:T(8,128)(2,1)} %bitcast.201, f32[4,2,2,8,128]{4,3,2,1,0:T(8,128)} %stack.132.gains), custom_call_target="tpu_custom_call" | custom-call | tf_op jit(solution)/shard_map/attn_grads/pallas_call | solution.py:912
  (303 shorter events, 90.7 us)
Async XLA Ops:
  114.3 10.3 %copy-start.14 = (f32[256,768]{1,0:T(8,128)}, f32[256,768]{1,0:T(8,128)S(1)}, u32[]{:S(2)}) copy-start(f32[256,768]{1,0:T(8,128)S(1)} %fusion.80) | copy-start | bytes 2359300
  116.2 3.9 copy-start.48
  116.2 3.9 copy-start.46
  119.5 4.9 copy-start.65
  120.7 3.9 copy-start.36
  120.7 3.9 copy-start.38
  127.9 389.1 %copy-start.56 = (f32[256]{0:T(256)}, f32[256]{0:T(256)S(1)}, u32[]{:S(2)}) copy-start(f32[256]{0:T(256)S(1)} %fusion.70) | copy-start | bytes 3076
  174.5 6.0 copy-start.25
  174.5 6.1 copy-start.23
  180.6 8.6 %copy-start.82 = (f32[2048,864]{0,1:T(8,128)}, f32[2048,864]{0,1:T(8,128)S(1)}, u32[]{:S(2)}) copy-start(f32[2048,864]{0,1:T(8,128)S(1)} %fusion.88) | copy-start | bytes 21233668
  180.6 8.6 %copy-start.80 = (bf16[2,432,1152]{2,1,0:T(8,128)(2,1)S(1)}, bf16[2,432,1152]{2,1,0:T(8,128)(2,1)}, u32[]{:S(2)}) copy-start(bf16[2,432,1152]{2,1,0:T(8,128)(2,1)} %get-tuple-element.29) | copy-start | bytes 5971972
  189.2 7.7 %copy-start.83 = (bf16[2048,864]{0,1:T(8,128)(2,1)}, bf16[2048,864]{0,1:T(8,128)(2,1)S(1)}, u32[]{:S(2)}) copy-start(bf16[2048,864]{0,1:T(8,128)(2,1)S(1)} %get-tuple-element.92) | copy-start | bytes 10616836
  196.9 37.7 %copy-start.53 = (f32[4,2,2,72]{3,2,1,0:T(2,128)S(1)}, f32[4,2,2,72]{3,2,1,0:T(2,128)}, u32[]{:S(2)}) copy-start(f32[4,2,2,72]{3,2,1,0:T(2,128)} %get-tuple-element.47) | copy-start | bytes 13828
  271.3 9.6 %copy-start.13 = (bf16[8,256,1152]{2,1,0:T(8,128)(2,1)S(1)}, bf16[8,256,1152]{2,1,0:T(8,128)(2,1)}, u32[]{:S(2)}) copy-start(bf16[8,256,1152]{2,1,0:T(8,128)(2,1)} %cube_gather.3) | copy-start | bytes 14155780
  271.3 9.6 %copy-start.81 = (bf16[2,432,1152]{2,1,0:T(8,128)(2,1)S(1)}, bf16[2,432,1152]{2,1,0:T(8,128)(2,1)}, u32[]{:S(2)}) copy-start(bf16[2,432,1152]{2,1,0:T(8,128)(2,1)} %get-tuple-element.29) | copy-start | bytes 5971972
  271.3 24.2 %slice-start = ((s8[4718592]{0:T(1024)(128)(4,1)}), s8[4194304]{0:T(1024)(128)(4,1)S(1)}, s32[]{:S(2)}) async-start(s8[4718592]{0:T(1024)(128)(4,1)} %bitcast.218), calls=%async_computation | async-start | bytes 8388608
  280.9 14.6 %slice-start.1 = ((s8[4718592]{0:T(1024)(128)(4,1)}), s8[524288]{0:T(1024)(128)(4,1)S(1)}, s32[]{:S(2)}) async-start(s8[4718592]{0:T(1024)(128)(4,1)} %bitcast.218), calls=%async_computation.1 | async-start | bytes 1048576
  461.3 7.8 %copy-start.24 = (bf16[1,4,2,2,72,864]{5,4,3,2,1,0:T(8,128)(2,1)S(1)}, bf16[1,4,2,2,72,864]{5,4,3,2,1,0:T(8,128)(2,1)}, u32[]{:S(2)}) copy-start(bf16[1,4,2,2,72,864]{5,4,3,2,1,0:T(8,128)(2,1)} %copy-done.23) | copy-start | bytes 5971972
  461.3 7.8 %copy-start.85 = (bf16[2048,864]{0,1:T(8,128)(2,1)S(1)}, bf16[2048,864]{0,1:T(8,128)(2,1)}, u32[]{:S(2)}) copy-start(bf16[2048,864]{0,1:T(8,128)(2,1)} %get-tuple-element.56) | copy-start | bytes 10616836
  520.5 3.8 copy-start.64
  620.6 4.2 copy-start.79
  620.6 5.3 copy-start.73
  620.6 5.3 copy-start.4
  620.6 5.3 copy-start.11
  (64 other events, 120.6 us)

commit v2 on v0

--- a/solution.py
+++ b/solution.py
@@ -4,6 +4,8 @@
 import jax
 import jax.numpy as jnp
 from jax import lax
+from jax.experimental import pallas as pl
+from jax.experimental.pallas import tpu as pltpu
 from jax.sharding import PartitionSpec as P
 
 EPS = 1e-06
@@ -90,7 +92,7 @@
     return jnp.broadcast_to(values[:, None], (values.shape[0], lax.axis_size("replica")))
 
 
-def body(
+def general_body(
     layer_in,
     d_out,
     segments,
@@ -348,6 +350,1120 @@
     )
 
 
+MESH = pl.DeviceIdType.MESH
+VMEM_BYTES = 60 * 2**20
+F32 = jnp.float32
+BF16 = jnp.bfloat16
+
+
+def fits_cubes(mesh):
+    return dict(mesh.shape) == {"replica": 2, "fsdp": 16}
+
+
+class Place:
+    def __init__(self):
+        shard = lax.axis_index("fsdp")
+        self.x = lax.axis_index("replica")
+        self.shard = shard
+        self.c = lax.rem(shard, 2)
+        self.y = lax.rem(lax.div(shard, 2), 2)
+        self.z = lax.div(shard, 4)
+        self.zl = lax.rem(self.z, 2)
+        self.zh = lax.div(self.z, 2)
+
+    def at(self, x=None, y=None, z=None, c=None):
+        x = self.x if x is None else x
+        y = self.y if y is None else y
+        z = self.z if z is None else z
+        c = self.c if c is None else c
+        return (x, (z * 2 + y) * 2 + c)
+
+    def z_xor(self, k):
+        low = self.zl if k % 2 == 0 else 1 - self.zl
+        high = self.zh if k // 2 == 0 else 1 - self.zh
+        return 2 * high + low
+
+    def cube(self, bits):
+        return self.at(
+            x=1 - self.x if bits & 4 else self.x,
+            y=1 - self.y if bits & 2 else self.y,
+            z=self.z_xor(1) if bits & 1 else self.z,
+        )
+
+
+class Wires:
+    def __init__(self, send, recv):
+        self.send, self.recv, self.used = send, recv, 0
+
+    def remote(self, src, dst, device):
+        i = self.used
+        self.used += 1
+        return pltpu.make_async_remote_copy(
+            src_ref=src,
+            dst_ref=dst,
+            send_sem=self.send.at[i],
+            recv_sem=self.recv.at[i],
+            device_id=device,
+            device_id_type=MESH,
+        )
+
+    def local(self, src, dst):
+        i = self.used
+        self.used += 1
+        return pltpu.make_async_copy(src, dst, self.send.at[i])
+
+
+def greet(devices):
+    barrier = pltpu.get_barrier_semaphore()
+    for device in devices:
+        pl.semaphore_signal(barrier, inc=1, device_id=device, device_id_type=MESH)
+    pl.semaphore_wait(barrier, len(devices))
+
+
+def hbm():
+    return pl.BlockSpec(memory_space=pl.ANY)
+
+
+def vmem():
+    return pl.BlockSpec(memory_space=pltpu.VMEM)
+
+
+def sems(count):
+    return [pltpu.SemaphoreType.DMA((count,)), pltpu.SemaphoreType.DMA((count,))]
+
+
+def params(collective_id):
+    return pltpu.CompilerParams(
+        collective_id=collective_id, has_side_effects=True, vmem_limit_bytes=VMEM_BYTES
+    )
+
+
+X, Y, Z = 4, 2, 1
+
+
+def thirds(rows):
+    first = -(-rows // 48) * 16
+    return ((0, first), (first, first), (2 * first, rows - 2 * first))
+
+
+def cube_gather_kernel(block, every, send, recv, local):
+    p = Place()
+    w = Wires(send, recv)
+    greet([p.cube(X), p.cube(Y), p.cube(Z)])
+    started = []
+    for _ in cube_gather_steps(p, w, block, every, local.at[0], started):
+        pass
+    for copy in started:
+        copy.wait_send()
+
+
+def cube_gather(block):
+    return pl.pallas_call(
+        cube_gather_kernel,
+        out_shape=jax.ShapeDtypeStruct((8,) + block.shape, block.dtype),
+        in_specs=[hbm()],
+        out_specs=hbm(),
+        scratch_shapes=sems(24) + [pltpu.SemaphoreType.DMA((1,))],
+        compiler_params=params(1),
+        name="cube_gather",
+    )(block)
+
+
+def cube_sum_kernel(parts, total, ready, third, second, first, send, recv):
+    p = Place()
+    w = Wires(send, recv)
+    near = {bit: p.cube(bit) for bit in (X, Y, Z)}
+    greet([near[X], near[Y], near[Z]])
+    started = []
+
+    def push(src, dst, bit):
+        copy = w.remote(src, dst, near[bit])
+        copy.start()
+        started.append(copy)
+        return copy
+
+    rows = total.shape[0]
+    half = rows // 2
+    far, mid, end = {}, {}, {}
+    for h in range(2):
+        for (start, size), link in zip(thirds(half), (X, Y, Z)):
+            at = pl.ds(h * half + start, size)
+            far[link, h] = push(parts.at[7, at], third.at[at], link)
+    for h in range(2):
+        for i, (link, onward, place) in enumerate(((X, Y, Y | Z), (Y, Z, X | Z), (Z, X, X | Y))):
+            start, size = thirds(half)[i]
+            at = pl.ds(h * half + start, size)
+            all_at = pl.ds(h * half, half)
+            far[link, h].wait_recv()
+            ready[i, all_at] = parts[place, all_at]
+            ready[i, at] = (parts[place, at].astype(F32) + third[at].astype(F32)).astype(BF16)
+            mid[onward, h] = push(ready.at[i, all_at], second.at[i, all_at], onward)
+    for h in range(2):
+        at = pl.ds(h * half, half)
+        for i, (came, place) in enumerate(((Y, Z), (Z, X), (X, Y))):
+            mid[came, h].wait_recv()
+            ready[3 + i, at] = (parts[place, at].astype(F32) + second[i, at].astype(F32)).astype(BF16)
+            end[place, h] = push(ready.at[3 + i, at], first.at[i, at], place)
+    for h in range(2):
+        at = pl.ds(h * half, half)
+        value = parts[0, at].astype(F32)
+        for i, place in enumerate((Z, X, Y)):
+            end[place, h].wait_recv()
+            value = value + first[i, at].astype(F32)
+        total[at, :] = value
+    for copy in started:
+        copy.wait_send()
+
+
+def cube_sum(parts):
+    _, rows, columns = parts.shape
+    return pl.pallas_call(
+        cube_sum_kernel,
+        out_shape=jax.ShapeDtypeStruct((rows, columns), F32),
+        in_specs=[vmem()],
+        out_specs=vmem(),
+        scratch_shapes=[
+            pltpu.VMEM((6, rows, columns), BF16),
+            pltpu.VMEM((rows, columns), BF16),
+            pltpu.VMEM((3, rows, columns), BF16),
+            pltpu.VMEM((3, rows, columns), BF16),
+        ]
+        + sems(24),
+        compiler_params=params(2),
+        name="cube_sum",
+    )(parts)
+
+
+def add(left, right):
+    return (left.astype(F32) + right.astype(F32)).astype(BF16)
+
+
+def norm_scale(values):
+    return lax.rsqrt(jnp.mean(values * values, axis=-1, keepdims=True) + EPS)
+
+
+def norm_pull(values, scale, gain, cotangent):
+    weighted = gain * cotangent
+    lean = jnp.mean(values * weighted, axis=-1, keepdims=True)
+    d_values = scale * weighted - values * (scale * scale * scale * lean)
+    return d_values, jnp.sum(values * scale * cotangent, axis=0, keepdims=True)
+
+
+def spread_matrix(width, per):
+    column = lax.broadcasted_iota(jnp.int32, (128, width), 1)
+    row = lax.broadcasted_iota(jnp.int32, (128, width), 0)
+    place = (lax.rem(column, per) == row).astype(F32)
+    column = lax.broadcasted_iota(jnp.int32, (16, width), 1)
+    row = lax.broadcasted_iota(jnp.int32, (16, width), 0)
+    owner = (lax.div(column, per) == row).astype(F32)
+    return place, owner
+
+
+def join_gains(packed, which, width, per):
+    place, owner = spread_matrix(width, per)
+    shards = packed[:, which, :].astype(BF16)
+    wide = jnp.dot(shards, place.astype(BF16), preferred_element_type=F32)
+    return jnp.sum(wide * owner, axis=0, keepdims=True)
+
+
+def turn(values, cosine, sine):
+    half = values.shape[-1] // 2
+    u, w = values[:, :half], values[:, half:]
+    return jnp.concatenate([u * cosine - w * sine, w * cosine + u * sine], axis=1)
+
+
+def turn_back(values, cosine, sine):
+    half = values.shape[-1] // 2
+    u, w = values[:, :half], values[:, half:]
+    return jnp.concatenate([u * cosine + w * sine, w * cosine - u * sine], axis=1)
+
+
+def front_kernel(
+    tok, seg_row, seg_col, w_q, w_k, w_v, w_o, gains, w_gate, w_up, w_down,
+    qkv_w, out_w, gu_w, dn_w, every, gains_full, a_low, qk_proj, q_low, k_low, v_low,
+    probs, o_low, attn_proj, h_mid, tables,
+    qkv_s, qkv_own, qkv_send, qkv_got, out_own, gains_own, gains_s, wide_in, wide_send, wide_got,
+    wide_out, down_in, down_out, m_low, out_s, send, recv, local,
+):
+    p = Place()
+    w = Wires(send, recv)
+    x, y, z, c, zl, zh = p.x, p.y, p.z, p.c, p.zl, p.zh
+    sibling = p.at(c=1 - c)
+    plane = [p.at(x=1 - x), p.at(y=1 - y)]
+    lines = [p.at(y=yy, z=p.z_xor(k)) for yy in (y, 1 - y) for k in range(1, 4)]
+    started = []
+
+    def push(src, dst, device):
+        copy = w.remote(src, dst, device)
+        copy.start()
+        started.append(copy)
+        return copy
+
+    loads = [
+        pltpu.make_async_copy(w_gate, wide_in.at[0], local.at[0]),
+        pltpu.make_async_copy(w_up, wide_in.at[1], local.at[1]),
+        pltpu.make_async_copy(w_down, down_in, local.at[2]),
+    ]
+    for copy in loads:
+        copy.start()
+
+    rows = w_q.shape[0]
+    columns = qkv_s.shape[1] // 4
+    out_rows = w_o.shape[0] // 2
+    mine = 2 * x + c
+    theirs = 2 * x + 1 - c
+
+    all_own = jnp.concatenate([w_q[...], w_k[...], w_v[...]], axis=1)
+    for quarter in range(4):
+        qkv_own[quarter] = all_own[:, quarter * columns : (quarter + 1) * columns]
+    qkv_send[...] = qkv_own[theirs].astype(BF16)
+    out_own[...] = w_o[...].astype(BF16)
+    gains_own[...] = gains[...].astype(BF16).astype(F32)
+    greet([sibling] + plane + lines)
+
+    def qkv_at(zz, yy, quarter):
+        return qkv_s.at[
+            pl.ds(pl.multiple_of((2 * zz + yy) * 2 * rows, 16), 2 * rows),
+            pl.ds(pl.multiple_of(quarter * columns, 128), columns),
+        ]
+
+    def out_at(zz, yy, quarter):
+        return out_s.at[
+            pl.ds(pl.multiple_of((2 * zz + yy) * 4 * out_rows + quarter * out_rows, 16), out_rows)
+        ]
+
+    swap = push(qkv_send, qkv_got, sibling)
+
+    def gains_at(zz, yy, cc):
+        return gains_s.at[(2 * zz + yy) * 2 + cc]
+
+    gains_s[(2 * z + y) * 2 + c] = gains_own[...]
+    gain_line = [push(gains_own, gains_at(z, y, c), p.at(z=p.z_xor(k))) for k in range(1, 4)]
+    gain_side = [push(gains_own, gains_at(z, y, c), plane[1])]
+    holds = x == c
+    out_theirs = out_own.at[pl.ds(pl.multiple_of((1 - c) * out_rows, 16), out_rows)]
+    out_swap = w.remote(out_theirs, out_at(z, y, theirs), sibling)
+    pl.when(holds)(out_swap.start)
+
+    @pl.when(holds)
+    def _():
+        out_s[pl.ds(pl.multiple_of((2 * z + y) * 4 * out_rows + mine * out_rows, 16), out_rows)] = (
+            out_own[pl.ds(pl.multiple_of(c * out_rows, 16), out_rows)]
+        )
+
+    swap.wait_recv()
+    top, low = qkv_own[mine], qkv_got[...].astype(F32)
+    first = jnp.where(c == 0, top, low)
+    second = jnp.where(c == 0, low, top)
+    base = pl.multiple_of((2 * z + y) * 2 * rows, 16)
+    joined = jnp.concatenate([first, second], axis=0).astype(BF16)
+    qkv_s[pl.ds(base, 2 * rows), pl.ds(pl.multiple_of(mine * columns, 128), columns)] = joined
+
+    pl.when(jnp.logical_not(holds))(out_swap.wait_recv)
+    pl.when(holds)(out_swap.wait_send)
+
+    line = [None]
+    for k in range(1, 4):
+        to = p.at(z=p.z_xor(k))
+        line.append(
+            (
+                push(qkv_at(z, y, mine), qkv_at(z, y, mine), to),
+                push(out_at(z, y, mine), out_at(z, y, mine), to),
+            )
+        )
+    side_x, side_y, corner = {}, {}, {}
+
+    def spread(k):
+        zz = p.z_xor(k)
+        if k:
+            for copy in line[k]:
+                copy.wait_recv()
+        qkv, out = qkv_at(zz, y, mine), out_at(zz, y, mine)
+        side_x[k] = (push(qkv, qkv, plane[0]), push(out, out, plane[0]))
+        side_y[k] = (push(qkv, qkv, plane[1]), push(out, out, plane[1]))
+
+    def relay(k):
+        zz = p.z_xor(k)
+        if k % 2:
+            for copy in side_y[k]:
+                copy.wait_recv()
+            qkv, out, to = qkv_at(zz, 1 - y, mine), out_at(zz, 1 - y, mine), plane[0]
+        else:
+            for copy in side_x[k]:
+                copy.wait_recv()
+            other = 2 * (1 - x) + c
+            qkv, out, to = qkv_at(zz, y, other), out_at(zz, y, other), plane[1]
+        corner[k] = (push(qkv, qkv, to), push(out, out, to))
+
+    pairs = []
+
+    def share(k):
+        zz = p.z_xor(k)
+        for copy in (side_x[k] if k % 2 else side_y[k]) + corner[k]:
+            copy.wait_recv()
+        for xx in range(2):
+            at = qkv_s.at[
+                pl.ds(pl.multiple_of(2 * zz * 2 * rows, 16), 4 * rows),
+                pl.ds(pl.multiple_of((2 * xx + c) * columns, 128), columns),
+            ]
+            pairs.append(push(at, at, sibling))
+            for yy in range(2):
+                at = out_at(zz, yy, 2 * xx + c)
+                pairs.append(push(at, at, sibling))
+
+    spread(0)
+    loads[0].wait()
+    loads[1].wait()
+    part_columns = wide_out.shape[-1]
+    for xx in range(2):
+
+        @pl.when(x == xx)
+        def _():
+            for zz in range(2):
+                for yy in range(2):
+                    part = (2 * zz + xx) * 2 + yy
+                    at = slice(part * part_columns, (part + 1) * part_columns)
+                    for matrix in range(2):
+
+                        @pl.when(c == 1 - matrix)
+                        def _():
+                            wide_send[2 * zz + yy] = wide_in[matrix, :, at].astype(BF16)
+
+    wide_swap = push(wide_send, wide_got, sibling)
+    loads[2].wait()
+    down_out[...] = down_in[...].astype(BF16)
+    relay(0)
+    spread(1)
+    wide_swap.wait_recv()
+    for xx in range(2):
+
+        @pl.when(x == xx)
+        def _():
+            for zz in range(2):
+                for yy in range(2):
+                    part = (2 * zz + xx) * 2 + yy
+                    at = slice(part * part_columns, (part + 1) * part_columns)
+                    got = wide_got[2 * zz + yy].astype(F32)
+                    for matrix in range(2):
+
+                        @pl.when(c == matrix)
+                        def _():
+                            own = wide_in[matrix, :, at]
+                            both = [own, got] if matrix == 0 else [got, own]
+                            wide_out[2 * zz + yy] = jnp.concatenate(both, axis=0).astype(BF16)
+
+    def gu_at(zz, yy):
+        return gu_w.at[c, pl.ds(pl.multiple_of((2 * zz + yy) * 2 * rows, 16), 2 * rows)]
+
+    wide = []
+    for k in (3, 2, 1, 0):
+        for other in (1, 0):
+            yy = 1 - y if other else y
+            zz = p.z_xor(k)
+            src = wide_out.at[2 * lax.rem(zz, 2) + yy]
+            if k == 0 and other == 0:
+                own_wide = pltpu.make_async_copy(src, gu_at(z, y), local.at[0])
+                own_wide.start()
+            else:
+                wide.append((zz, yy, push(src, gu_at(z, y), p.at(y=yy, z=zz))))
+    down_rows = down_out.shape[0]
+    down_at = dn_w.at[pl.ds(pl.multiple_of(c * down_rows, 16), down_rows)]
+    source_z = 2 * zl + x
+    first_down = w.used
+    w.used += 2
+    down_sends = []
+    for half in range(2):
+        zz = 2 * half + zh
+        copy = pltpu.make_async_remote_copy(
+            src_ref=down_out,
+            dst_ref=down_at,
+            send_sem=send.at[first_down + half],
+            recv_sem=recv.at[first_down],
+            device_id=p.at(z=zz),
+            device_id_type=MESH,
+        )
+        need = (x == zl) & (zz != z)
+        pl.when(need)(copy.start)
+        down_sends.append((need, copy))
+    own_down = pltpu.make_async_copy(down_out, down_at, local.at[1])
+    pl.when(source_z == z)(own_down.start)
+
+    tok_f = tok[...].astype(F32)
+    length, width = tok_f.shape
+    head = k_low.shape[1]
+    spread(2)
+    relay(1)
+    for copy in gain_line:
+        copy.wait_recv()
+    for k in range(1, 4):
+        zz = p.z_xor(k)
+        gain_side.append(push(gains_at(zz, y, c), gains_at(zz, y, c), plane[1]))
+    row_seg = seg_row[...].astype(F32)
+    col_seg = seg_col[...].astype(F32)
+    earlier = jnp.sum((row_seg < col_seg).astype(F32), axis=1, keepdims=True)
+    index = lax.broadcasted_iota(jnp.int32, (length, 1), 0).astype(F32)
+    rate_at = lax.broadcasted_iota(jnp.int32, (1, head // 2), 1).astype(F32)
+    rates = jnp.exp(rate_at * (-2.0 * math.log(THETA) / head))
+    angles = (index - earlier) * rates
+    tables[0] = jnp.cos(angles)
+    tables[1] = jnp.sin(angles)
+    spread(3)
+    relay(2)
+    share(0)
+    relay(3)
+    for copy in gain_side:
+        copy.wait_recv()
+    gain_pair = []
+    for zz in range(4):
+        for yy in range(2):
+            gain_pair.append(push(gains_at(zz, yy, c), gains_at(zz, yy, c), sibling))
+    share(1)
+    for copy in gain_pair:
+        copy.wait_recv()
+    packed = gains_s[...]
+    for i, (size, per) in enumerate(
+        ((width, rows),) * 4 + ((head, head // 16),) * 2
+    ):
+        gains_full[i, :, :size] = join_gains(packed, i, size, per)
+    a_low[...] = (tok_f * norm_scale(tok_f) * gains_full[0]).astype(BF16)
+    share(2)
+    share(3)
+    for copy in pairs:
+        copy.wait_recv()
+    saves = [
+        pltpu.make_async_copy(qkv_s, qkv_w, local.at[2]),
+        pltpu.make_async_copy(out_s, out_w, local.at[3]),
+    ]
+    for copy in saves:
+        copy.start()
+
+    cosine, sine = tables[0], tables[1]
+    heads = q_low.shape[1] // head
+    for i in range(heads + 2):
+        at = slice(i * head, (i + 1) * head)
+        value = jnp.dot(a_low[...], qkv_s[:, at], preferred_element_type=F32)
+        if i < heads:
+            qk_proj[:, at] = value
+            q_low[:, at] = turn(
+                value * norm_scale(value) * gains_full[4, :, :head], cosine, sine
+            ).astype(BF16)
+        elif i == heads:
+            qk_proj[:, at] = value
+            k_low[...] = turn(
+                value * norm_scale(value) * gains_full[5, :, :head], cosine, sine
+            ).astype(BF16)
+        else:
+            v_low[...] = value.astype(BF16)
+    i_at = lax.broadcasted_iota(jnp.int32, (length, length), 0)
+    j_at = lax.broadcasted_iota(jnp.int32, (length, length), 1)
+    allowed = (row_seg == col_seg) & (j_at <= i_at)
+    for i in range(heads):
+        at = slice(i * head, (i + 1) * head)
+        scores = SCALE * lax.dot_general(
+            q_low[:, at], k_low[...], (((1,), (1,)), ((), ())), preferred_element_type=F32
+        )
+        scores = jnp.where(allowed, scores, MASKED)
+        expo = jnp.exp(scores - jnp.max(scores, axis=1, keepdims=True))
+        prob = expo / jnp.sum(expo, axis=1, keepdims=True)
+        probs[i] = prob
+        o_low[:, at] = jnp.dot(
+            prob.astype(BF16), v_low[...], preferred_element_type=F32
+        ).astype(BF16)
+    third = width // 3
+    for i in range(3):
+        at = slice(i * third, (i + 1) * third)
+        attn_proj[:, at] = jnp.dot(o_low[...], out_s[:, at], preferred_element_type=F32)
+    proj = attn_proj[...]
+    mid = tok_f + proj * norm_scale(proj) * gains_full[1]
+    h_mid[...] = mid
+    m_low[...] = (mid * norm_scale(mid) * gains_full[2]).astype(BF16)
+
+    finish = cube_gather_steps(p, w, m_low, every, local.at[4], started)
+    next(finish)
+    own_wide.wait()
+    shared = [push(gu_at(z, y), gu_at(z, y), sibling)]
+    next(finish)
+    for zz, yy, copy in reversed(wide):
+        copy.wait_recv()
+        shared.append(push(gu_at(zz, yy), gu_at(zz, yy), sibling))
+    next(finish)
+    pl.when(source_z == z)(own_down.wait)
+    pl.when(source_z != z)(down_sends[0][1].wait_recv)
+    shared.append(push(down_at, down_at, sibling))
+    for _ in finish:
+        pass
+    for copy in shared:
+        copy.wait_recv()
+    for copy in saves:
+        copy.wait()
+    for need, copy in down_sends:
+        pl.when(need)(copy.wait_send)
+    for copy in started:
+        copy.wait_send()
+
+
+def cube_gather_steps(p, w, block, every, own_sem, started):
+    near = {bit: p.cube(bit) for bit in (X, Y, Z)}
+
+    def push(src, dst, bit):
+        copy = w.remote(src, dst, near[bit])
+        copy.start()
+        started.append(copy)
+        return copy
+
+    rows = block.shape[0]
+    half = rows // 2
+    own = pltpu.make_async_copy(block, every.at[0], own_sem)
+    own.start()
+    arrivals = {}
+    for h in range(2):
+        at = pl.ds(h * half, half)
+        for bit in (X, Y, Z):
+            arrivals[bit, h] = push(block.at[at], every.at[bit, at], bit)
+    yield
+    for h in range(2):
+        at = pl.ds(h * half, half)
+        for link, relay in ((X, Y), (Y, Z), (Z, X)):
+            arrivals[relay, h].wait_recv()
+            arrivals[link | relay, h] = push(every.at[relay, at], every.at[link | relay, at], link)
+    yield
+    last = []
+    for h in range(2):
+        for (start, size), link, relay in zip(thirds(half), (X, Y, Z), (Y | Z, X | Z, X | Y)):
+            at = pl.ds(h * half + start, size)
+            arrivals[relay, h].wait_recv()
+            last.append(push(every.at[relay, at], every.at[7, at], link))
+    yield
+    for copy in last:
+        copy.wait_recv()
+    own.wait()
+
+
+def front(tok, segments, w_q, w_k, w_v, w_o, gains, w_gate, w_up, w_down, head):
+    length, width = tok.shape
+    rows, mix = w_q.shape
+    hidden = w_gate.shape[1]
+    part = hidden // 8
+    down_rows = w_down.shape[0]
+    total = mix + 2 * head
+    heads = mix // head
+    columns = total // 4
+    struct = jax.ShapeDtypeStruct
+    shapes = (
+        struct((16 * rows, total), BF16),
+        struct((16 * w_o.shape[0], width), BF16),
+        struct((2, 16 * rows, part), BF16),
+        struct((2 * down_rows, width), BF16),
+        struct((8, length, width), BF16),
+        struct((8, 1, width), F32),
+        struct((length, width), BF16),
+        struct((length, mix + head), F32),
+        struct((length, mix), BF16),
+        struct((length, head), BF16),
+        struct((length, head), BF16),
+        struct((heads, length, length), F32),
+        struct((length, mix), BF16),
+        struct((length, width), F32),
+        struct((length, width), F32),
+        struct((2, length, head // 2), F32),
+    )
+    scratch = [
+        pltpu.VMEM((16 * rows, total), BF16),
+        pltpu.VMEM((4, rows, columns), F32),
+        pltpu.VMEM((rows, columns), BF16),
+        pltpu.VMEM((rows, columns), BF16),
+        pltpu.VMEM(w_o.shape, BF16),
+        pltpu.VMEM(gains.shape, F32),
+        pltpu.VMEM((16,) + gains.shape, F32),
+        pltpu.VMEM((2, rows, hidden), F32),
+        pltpu.VMEM((4, rows, part), BF16),
+        pltpu.VMEM((4, rows, part), BF16),
+        pltpu.VMEM((4, 2 * rows, part), BF16),
+        pltpu.VMEM((down_rows, width), F32),
+        pltpu.VMEM((down_rows, width), BF16),
+        pltpu.VMEM((length, width), BF16),
+        pltpu.VMEM((16 * w_o.shape[0], width), BF16),
+    ]
+    return pl.pallas_call(
+        front_kernel,
+        out_shape=shapes,
+        in_specs=[vmem()] * 8 + [hbm()] * 3,
+        out_specs=(hbm(),) * 5 + (vmem(),) * 11,
+        scratch_shapes=scratch + sems(128) + [pltpu.SemaphoreType.DMA((5,))],
+        compiler_params=params(0),
+        name="front",
+    )(
+        tok, segments, segments.reshape(-1, 1), w_q, w_k, w_v, w_o, gains, w_gate, w_up, w_down
+    )
+
+
+def dot_rows(left, right):
+    return lax.dot_general(left, right, (((0,), (0,)), ((), ())), preferred_element_type=F32)
+
+
+def dot_columns(left, right):
+    return lax.dot_general(left, right, (((1,), (1,)), ((), ())), preferred_element_type=F32)
+
+
+def back_kernel(
+    tok, d_out, d_normed, gains_full, a_low, qk_proj, q_low, k_low, v_low, probs, o_low, attn_proj,
+    h_mid, tables, g_mpost, qkv_hbm, out_hbm, gu, dn,
+    grad_x, grad_qkv, grad_out, grad_gains, grad_gu, grad_dn,
+    qkv_w, out_w, wide_in, wide_got, wide_sum, wide_far, down_in, down_got, down_sum, down_far,
+    down_end, d_input, wide_end, wide_swap, wide_back, d_attn, d_mid, d_mix, d_qkv, dqkv, dout, q1, o1, q2, o2, q3, o3, qe, oe,
+    gain_acc, gain_got, send, recv, local,
+):
+    p = Place()
+    w = Wires(send, recv)
+    x, y, z, c, zl, zh = p.x, p.y, p.z, p.c, p.zl, p.zh
+    sibling = p.at(c=1 - c)
+    plane = [p.at(x=1 - x), p.at(y=1 - y), p.at(x=1 - x, y=1 - y)]
+    line = [p.at(z=p.z_xor(k)) for k in range(1, 4)]
+    cube = [p.cube(bits) for bits in range(1, 8)]
+    started = []
+
+    def push(src, dst, device):
+        copy = w.remote(src, dst, device)
+        copy.start()
+        started.append(copy)
+        return copy
+
+    def rows_of(ref, start, size):
+        return ref.at[pl.ds(pl.multiple_of(start, 16), size)]
+
+    loads = [
+        pltpu.make_async_copy(gu.at[c], wide_in, local.at[0]),
+        pltpu.make_async_copy(dn, down_in, local.at[1]),
+        pltpu.make_async_copy(out_hbm, out_w, local.at[2]),
+        pltpu.make_async_copy(qkv_hbm, qkv_w, local.at[3]),
+    ]
+    for copy in loads:
+        copy.start()
+    greet([sibling] + plane + line + [p.cube(5), p.cube(7), p.cube(3)])
+
+    width = tok.shape[1]
+    chip_rows = wide_in.shape[0] // 8
+    down_rows = down_sum.shape[0]
+    half_rows = 4 * chip_rows
+    far_half = half_rows * (1 - zh)
+    near_half = half_rows * zh
+    wide_one = [
+        push(rows_of(gu.at[1 - c], start, half_rows), rows_of(wide_got, start, half_rows), sibling)
+        for start in (far_half, near_half)
+    ]
+    down_one = push(rows_of(dn, down_rows * (1 - c), down_rows), down_got, sibling)
+
+    mid = h_mid[...]
+    d_value, g_mpre = norm_pull(mid, norm_scale(mid), gains_full[2], d_normed[...])
+    d_mid[...] = d_out[...].astype(F32) + d_value
+    proj = attn_proj[...]
+    d_value, g_apost = norm_pull(proj, norm_scale(proj), gains_full[1], d_mid[...])
+    d_attn[...] = d_value.astype(BF16)
+    gain_acc[0, 2:3, :] = g_mpre
+    gain_acc[0, 1:2, :] = g_apost
+
+    loads[0].wait()
+    loads[1].wait()
+    wide_one[0].wait_recv()
+    order = (3, 1, 2, 0)
+
+    def piece(i):
+        to_z = 1 - zl if i // 2 else zl
+        to_y = 1 - y if i % 2 else y
+        return (2 * to_z + to_y) * chip_rows
+
+    wide_two = {}
+    for i in order:
+        rows = pl.ds(pl.multiple_of(far_half + piece(i), 16), chip_rows)
+        at = pl.ds(i * chip_rows, chip_rows)
+        wide_sum[at, :] = add(wide_in[rows, :], wide_got[rows, :])
+        wide_two[i] = push(wide_sum.at[at], wide_far.at[at], line[1])
+    down_one.wait_recv()
+    down_sum[...] = add(down_in[pl.ds(pl.multiple_of(down_rows * c, 16), down_rows), :], down_got[...])
+    down_two = w.remote(down_sum, down_far, line[1])
+    mine = zl == zh
+    pl.when(zl != zh)(down_two.start)
+
+    third = width // 3
+    for i in range(3):
+        at = slice(i * third, (i + 1) * third)
+        dout[:, at] = dot_rows(o_low[...], d_attn[:, at]).astype(BF16)
+    out_rows = dout.shape[0] // 32
+    columns = dqkv.shape[1] // 4
+
+    def out_at(ref, zz, yy, quarter):
+        return rows_of(ref, (2 * zz + yy) * 4 * out_rows + quarter * out_rows, out_rows)
+
+    out_one = [
+        push(
+            out_at(dout, zz, yy, 2 * xx + 1 - c),
+            o1.at[xx, yy, pl.ds(zz * out_rows, out_rows)],
+            sibling,
+        )
+        for zz in range(4)
+        for yy in range(2)
+        for xx in range(2)
+    ]
+    loads[2].wait()
+    d_mix[...] = dot_columns(d_attn[...], out_w[...]).astype(BF16)
+
+    cosine, sine = tables[0], tables[1]
+    head = k_low.shape[1]
+    heads = q_low.shape[1] // head
+    d_k, d_v, g_q = 0.0, 0.0, 0.0
+    for i in range(heads):
+        at = slice(i * head, (i + 1) * head)
+        prob = probs[i]
+        d_probs = dot_columns(d_mix[:, at], v_low[...])
+        row_dot = jnp.sum(prob * d_probs, axis=1, keepdims=True)
+        d_scores = (prob * (d_probs - row_dot)).astype(BF16)
+        d_q = SCALE * jnp.dot(d_scores, k_low[...], preferred_element_type=F32)
+        d_k = d_k + dot_rows(d_scores, q_low[:, at])
+        d_v = d_v + dot_rows(prob.astype(BF16), d_mix[:, at])
+        value = qk_proj[:, at]
+        d_value, gain = norm_pull(
+            value, norm_scale(value), gains_full[4, :, :head], turn_back(d_q, cosine, sine)
+        )
+        g_q = g_q + gain
+        d_qkv[:, at] = d_value.astype(BF16)
+    at = slice(heads * head, (heads + 1) * head)
+    value = qk_proj[:, at]
+    d_value, g_k = norm_pull(
+        value, norm_scale(value), gains_full[5, :, :head], turn_back(SCALE * d_k, cosine, sine)
+    )
+    d_qkv[:, at] = d_value.astype(BF16)
+    d_qkv[:, (heads + 1) * head :] = d_v.astype(BF16)
+    gain_acc[0, 4:5, :] = jnp.zeros((1, width), F32)
+    gain_acc[0, 5:8, :] = jnp.zeros((3, width), F32)
+    gain_acc[0, 4:5, :head] = g_q
+    gain_acc[0, 5:6, :head] = g_k
+    for i in range(heads + 2):
+        at = slice(i * head, (i + 1) * head)
+        dqkv[:, at] = dot_rows(a_low[...], d_qkv[:, at]).astype(BF16)
+
+    def qkv_columns(ref, quarter):
+        return ref.at[:, pl.ds(pl.multiple_of(quarter * columns, 128), columns)]
+
+    qkv_one = [push(qkv_columns(dqkv, 2 * xx + 1 - c), q1.at[xx], sibling) for xx in range(2)]
+
+    loads[3].wait()
+    tok_f = tok[...].astype(F32)
+    for i in range(3):
+        at = slice(i * third, (i + 1) * third)
+        d_input[:, at] = dot_columns(d_qkv[...], qkv_w[at, :])
+    d_value, g_apre = norm_pull(tok_f, norm_scale(tok_f), gains_full[0], d_input[...])
+    grad_x[...] = (d_mid[...] + d_value).astype(BF16)
+    gain_acc[0, 0:1, :] = g_apre
+    gain_acc[0, 3:4, :] = g_mpost[...]
+    gain_one = push(gain_acc.at[0], gain_got.at[0], sibling)
+
+    for copy in out_one + qkv_one:
+        copy.wait_recv()
+
+    def plane_part(xx, yy, q_ref, o_ref):
+        at = pl.ds(pl.multiple_of((2 * xx + c) * columns, 128), columns)
+        for zz in range(4):
+            rows = pl.ds(pl.multiple_of((2 * zz + yy) * chip_rows, 16), chip_rows)
+            q_ref[zz * chip_rows : (zz + 1) * chip_rows, :] = add(dqkv[rows, at], q1[xx, rows, :])
+            start = pl.multiple_of(((2 * zz + yy) * 4 + 2 * xx + c) * out_rows, 16)
+            here = slice(zz * out_rows, (zz + 1) * out_rows)
+            o_ref[here, :] = add(dout[pl.ds(start, out_rows), :], o1[xx, yy, here, :])
+
+    second = {}
+    for i in (2, 0, 1):
+        plane_part(x if i == 1 else 1 - x, y if i == 0 else 1 - y, q2.at[i], o2.at[i])
+        second[i] = (push(q2.at[i], q2.at[3 + i], plane[i]), push(o2.at[i], o2.at[3 + i], plane[i]))
+    gain_one.wait_recv()
+    gain_acc[1] = gain_acc[0] + gain_got[0]
+    gain_two = [push(gain_acc.at[1], gain_got.at[1 + i], plane[i]) for i in range(3)]
+    plane_part(x, y, q3, o3)
+
+    part = (2 * zl + x) * 2 + y
+    wide_three, own_wide = [], []
+
+    def wide_on(i):
+        at = pl.ds(i * chip_rows, chip_rows)
+        rows = pl.ds(pl.multiple_of(near_half + piece(i), 16), chip_rows)
+        wide_two[i].wait_recv()
+        own = wide_in[rows, :].astype(F32) + wide_got[rows, :].astype(F32)
+        wide_far[at, :] = (own + wide_far[at, :].astype(F32)).astype(BF16)
+        for over in (1, 0):
+            bits = 4 * over + 2 * (i % 2) + i // 2
+            if bits:
+                wide_three.append(push(wide_far.at[at], wide_end.at[part], p.cube(bits)))
+            else:
+                own_wide.append(
+                    pltpu.make_async_copy(wide_far.at[at], wide_end.at[part], local.at[4])
+                )
+                own_wide[0].start()
+
+    wide_one[1].wait_recv()
+    wide_on(3)
+    for i in range(3):
+        for copy in second[i]:
+            copy.wait_recv()
+    q3[...] = add(
+        q3[...].astype(F32) + q2[3].astype(F32), q2[4].astype(F32) + q2[5].astype(F32)
+    )
+    o3[...] = add(
+        o3[...].astype(F32) + o2[3].astype(F32), o2[4].astype(F32) + o2[5].astype(F32)
+    )
+    third_step = []
+    for k in range(1, 4):
+        zz = p.z_xor(k)
+        third_step += [
+            push(rows_of(q3, zz * chip_rows, chip_rows), qe.at[k], line[k - 1]),
+            push(rows_of(o3, zz * out_rows, out_rows), oe.at[k], line[k - 1]),
+        ]
+    for copy in gain_two:
+        copy.wait_recv()
+    gain_acc[2] = gain_acc[1] + gain_got[1] + gain_got[2] + gain_got[3]
+    gain_three = [push(gain_acc.at[2], gain_got.at[3 + k], line[k - 1]) for k in range(1, 4)]
+    wide_on(1)
+    for copy in third_step:
+        copy.wait_recv()
+    start = pl.multiple_of(z * chip_rows, 16)
+    qe[0] = add(
+        q3[pl.ds(start, chip_rows), :].astype(F32) + qe[1].astype(F32),
+        qe[2].astype(F32) + qe[3].astype(F32),
+    )
+    start = pl.multiple_of(z * out_rows, 16)
+    oe[0] = add(
+        o3[pl.ds(start, out_rows), :].astype(F32) + oe[1].astype(F32),
+        oe[2].astype(F32) + oe[3].astype(F32),
+    )
+    last = [
+        push(qe.at[0], qe.at[4 + i], device)
+        for i, device in enumerate((sibling, plane[0]))
+    ] + [
+        push(oe.at[0], oe.at[4 + i], device)
+        for i, device in enumerate((sibling, plane[0]))
+    ]
+    wide_on(2)
+    for copy in last:
+        copy.wait_recv()
+    relay = [push(qe.at[5], qe.at[6], sibling), push(oe.at[5], oe.at[6], sibling)]
+    wide_on(0)
+
+    arrive = w.used
+    w.used += 3
+    down_three = []
+    for xx in range(2):
+        copy = pltpu.make_async_remote_copy(
+            src_ref=down_far,
+            dst_ref=down_end,
+            send_sem=send.at[arrive + xx],
+            recv_sem=recv.at[arrive],
+            device_id=p.at(x=xx, z=2 * zh + x),
+            device_id_type=MESH,
+        )
+        down_three.append((mine & ((x != xx) | (zh != x)), copy))
+    down_here = mine & (x == zl)
+
+    @pl.when(mine)
+    def _():
+        down_two.wait_recv()
+        down_far[...] = add(down_sum[...], down_far[...])
+
+    down_own = pltpu.make_async_copy(down_far, down_end, local.at[5])
+    for need, copy in down_three:
+        pl.when(need)(copy.start)
+    pl.when(down_here)(down_own.start)
+
+    for copy in relay:
+        copy.wait_recv()
+    rows = chip_rows // 2
+    for xx in range(2):
+        for cc in range(2):
+
+            @pl.when((x == xx) & (c == cc))
+            def _():
+                for i, q in ((0, 2 * xx + cc), (4, 2 * xx + 1 - cc), (5, 2 * (1 - xx) + cc), (6, 2 * (1 - xx) + 1 - cc)):
+                    both = qe[i].astype(F32)
+                    grad_qkv[:, q * columns : (q + 1) * columns] = both[cc * rows : (cc + 1) * rows]
+                    if q // 2 == cc:
+                        grad_out[(q % 2) * out_rows : (q % 2 + 1) * out_rows, :] = oe[i].astype(F32)
+
+    for copy in gain_three:
+        copy.wait_recv()
+    grad_gains[...] = gain_acc[2] + gain_got[4] + gain_got[5] + gain_got[6]
+
+    own_wide[0].wait()
+    for copy in wide_three:
+        copy.wait_recv()
+    for cc in range(2):
+
+        @pl.when(c == cc)
+        def _():
+            for s in range(8):
+                extra = (rows + 15) // 16 * 16
+                at = slice(0, extra) if cc == 1 else slice(2 * rows - extra, 2 * rows)
+                wide_swap[s] = wide_end[s, at, :]
+
+    final = push(wide_swap, wide_back, sibling)
+    pl.when(down_here)(down_own.wait)
+    pl.when(jnp.logical_not(down_here))(down_three[0][1].wait_recv)
+    grad_dn[...] = down_end[...].astype(F32)
+    final.wait_recv()
+    for cc in range(2):
+
+        @pl.when(c == cc)
+        def _():
+            extra = (rows + 15) // 16 * 16
+            size = wide_end.shape[2]
+            for s in range(8):
+                at = slice(s * size, (s + 1) * size)
+                own = wide_end[s].astype(F32)[cc * rows : (cc + 1) * rows]
+                other = wide_back[s].astype(F32)
+                other = other[:rows] if cc == 0 else other[extra - rows :]
+                grad_gu[cc, :, at] = own
+                grad_gu[1 - cc, :, at] = other
+
+    for need, copy in down_three:
+        pl.when(need)(copy.wait_send)
+    pl.when(zl != zh)(down_two.wait_send)
+    for copy in started:
+        copy.wait_send()
+
+
+def back(
+    tok, d_out, d_normed, gains_full, saved, g_mpost, qkv_w, out_w, grad_gu, grad_dn, rows, out_rows
+):
+    length, width = tok.shape
+    total = qkv_w.shape[1]
+    columns = total // 4
+    mix = out_w.shape[0]
+    _, _, part = grad_gu.shape
+    down_rows = grad_dn.shape[0] // 2
+    chip_rows = 2 * rows
+    extra = (rows + 15) // 16 * 16
+    piece = out_rows // 2
+    struct = jax.ShapeDtypeStruct
+    shapes = (
+        struct((length, width), BF16),
+        struct((rows, total), F32),
+        struct((out_rows, width), F32),
+        struct((8, width), F32),
+        struct((2, rows, 8 * part), F32),
+        struct((down_rows, width), F32),
+    )
+    scratch = [
+        pltpu.VMEM(qkv_w.shape, BF16),
+        pltpu.VMEM(out_w.shape, BF16),
+        pltpu.VMEM((width, part), BF16),
+        pltpu.VMEM((width, part), BF16),
+        pltpu.VMEM((width // 2, part), BF16),
+        pltpu.VMEM((width // 2, part), BF16),
+        pltpu.VMEM(grad_dn.shape, BF16),
+        pltpu.VMEM((down_rows, width), BF16),
+        pltpu.VMEM((down_rows, width), BF16),
+        pltpu.VMEM((down_rows, width), BF16),
+        pltpu.VMEM((down_rows, width), BF16),
+        pltpu.VMEM((length, width), F32),
+        pltpu.VMEM((8, chip_rows, part), BF16),
+        pltpu.VMEM((8, extra, part), BF16),
+        pltpu.VMEM((8, extra, part), BF16),
+        pltpu.VMEM((length, width), BF16),
+        pltpu.VMEM((length, width), F32),
+        pltpu.VMEM((length, mix), BF16),
+        pltpu.VMEM((length, total), BF16),
+        pltpu.VMEM((width, total), BF16),
+        pltpu.VMEM((mix, width), BF16),
+        pltpu.VMEM((2, width, columns), BF16),
+        pltpu.VMEM((2, 2, 4 * piece, width), BF16),
+        pltpu.VMEM((6, 4 * chip_rows, columns), BF16),
+        pltpu.VMEM((6, 4 * piece, width), BF16),
+        pltpu.VMEM((4 * chip_rows, columns), BF16),
+        pltpu.VMEM((4 * piece, width), BF16),
+        pltpu.VMEM((7, chip_rows, columns), BF16),
+        pltpu.VMEM((7, piece, width), BF16),
+        pltpu.VMEM((3, 8, width), F32),
+        pltpu.VMEM((7, 8, width), F32),
+    ]
+    return pl.pallas_call(
+        back_kernel,
+        out_shape=shapes,
+        in_specs=[vmem()] * 15 + [hbm()] * 4,
+        out_specs=(vmem(),) * 6,
+        scratch_shapes=scratch + sems(96) + [pltpu.SemaphoreType.DMA((6,))],
+        compiler_params=params(3),
+        name="back",
+    )(tok, d_out, d_normed, gains_full, *saved, g_mpost, qkv_w, out_w, grad_gu, grad_dn)
+
+
+def pack_gains(vectors):
+    rows = [jnp.pad(v, (0, 128 - v.shape[0])) for v in vectors]
+    return jnp.concatenate(rows + [jnp.zeros(((8 - len(rows)) * 128,), F32)]).reshape(8, 128)
+
+
+def cube_body(
+    layer_in, d_out, segments, w_q, w_k, w_v, w_o, attn_pre, attn_post, q_gain, k_gain,
+    w_gate, w_up, w_down, mlp_pre, mlp_post,
+):
+    width = layer_in.shape[1]
+    head = q_gain.shape[0] * 16
+    rows, mix = w_q.shape
+    gain_list = [attn_pre, attn_post, mlp_pre, mlp_post, q_gain, k_gain]
+    (
+        qkv_w, out_w, gu_w, down_w, m_all, gains_full, a_low, qk_proj, q_low, k_low, v_low,
+        probs, o_low, attn_proj, h_mid, tables,
+    ) = front(
+        layer_in, segments, w_q, w_k, w_v, w_o, pack_gains(gain_list), w_gate, w_up, w_down, head
+    )
+    gate_w, up_w = gu_w[0], gu_w[1]
+    m_all = m_all.reshape(-1, width)
+    gate_val = matmul(m_all, gate_w)
+    up_val = matmul(m_all, up_w)
+    hidden, pull_h = jax.vjp(gelu_product, gate_val, up_val)
+    h_low = to_low(hidden)
+    down_val = cube_sum(to_low(matmul(h_low, down_w)).reshape(8, -1, width))
+    post_mlp, pull_pm = jax.vjp(norm_rows, down_val, gains_full[3, 0])
+    layer_out = (h_mid + post_mlp).astype(BF16)
+
+    d_down, g_mpost = pull_pm(d_out.astype(F32))
+    dd_all = cube_gather(to_low(d_down)).reshape(-1, width)
+    grad_wdown = to_low(matmul_left_t(h_low, dd_all))
+    d_hidden = matmul_right_t(dd_all, down_w)
+    d_gate, d_up = pull_h(d_hidden)
+    d_gate_low = to_low(d_gate)
+    d_up_low = to_low(d_up)
+    grad_gu = jnp.stack(
+        [to_low(matmul_left_t(m_all, d_gate_low)), to_low(matmul_left_t(m_all, d_up_low))]
+    )
+    d_normed = cube_sum(
+        to_low(matmul_right_t(d_gate_low, gate_w) + matmul_right_t(d_up_low, up_w)).reshape(
+            8, -1, width
+        )
+    )
+    saved = (a_low, qk_proj, q_low, k_low, v_low, probs, o_low, attn_proj, h_mid, tables)
+    grad_x, grad_qkv, grad_out, grad_gains, grad_gu, grad_dn = back(
+        layer_in, d_out, d_normed, gains_full, saved, g_mpost[None], qkv_w, out_w, grad_gu,
+        grad_wdown, rows, w_o.shape[0],
+    )
+    shard = lax.axis_index("fsdp")
+    g_apre, g_apost, g_mpre, g_mpost, g_q, g_k = [
+        lax.dynamic_slice(grad_gains[i], (shard * v.shape[0],), (v.shape[0],))
+        for i, v in enumerate(gain_list)
+    ]
+    return (
+        layer_out,
+        grad_x,
+        grad_qkv[:, :mix],
+        grad_qkv[:, mix : mix + head],
+        grad_qkv[:, mix + head :],
+        grad_out,
+        g_apre,
+        g_apost,
+        g_q,
+        g_k,
+        grad_gu[0],
+        grad_gu[1],
+        grad_dn,
+        g_mpre,
+        g_mpost,
+    )
+
+
 def solution(mesh):
     in_specs = (
         P(("replica", "fsdp"), None),
@@ -384,4 +1500,5 @@
         P("fsdp"),
         P("fsdp"),
     )
+    body = cube_body if fits_cubes(mesh) else general_body
     return jax.shard_map(body, mesh=mesh, in_specs=in_specs, out_specs=out_specs, check_vma=False)

time: 1970 us -> 478 us (0.24)
  waiting for transfers between devices: 1470 us -> 0 us
  Pallas kernels: 0 us -> 373 us
  blocking collectives: 242 us -> 0 us
  matrix products: 149 us -> 69.1 us
  other arithmetic: 46.5 us -> 8.63 us
    reduce_scatter x8 -> x0, waiting for transfers between devices: 1170 us -> none  [the longest x1 321 us: body(): lax.psum_scatter(grad_wgate, 'fsdp', scatter_dimension=0, tiled=True)]
    pallas_call x0 -> x5, Pallas kernels: none -> 373 us  [the longest x1 151 us: back(): pl.pallas_call(back_kernel, out_shape=shapes, in_specs=[vmem()] * 15 + [h...]
    all_gather x5 -> x0, waiting for transfers between devices: 296 us -> none  [the longest x1 109 us: body(): lax.all_gather(to_low(w_down), 'fsdp', axis=0, tiled=True)]
    all_gather x9 -> x0, blocking collectives: 130 us -> none  [the longest x1 24.7 us: body(): lax.all_gather(to_low(w_v), 'fsdp', axis=0, tiled=True)]
    unnamed x3 -> x0, blocking collectives: 113 us -> none
    dot_general x7 -> x3, matrix products: 51.5 us -> 19.9 us  [matmul_left_t(): lax.dot_general(left, right, (((0,), (0,)), ((), ())), preferred_element_...]
    dot_general x7 -> x3, matrix products: 50.5 us -> 25 us  [matmul_right_t(): lax.dot_general(left, right, (((1,), (1,)), ((), ())), preferred_element_...]
    unnamed x188 -> x41, local copies, waits for them, and re-layouts: 30.6 us -> 8.45 us
  transfers between devices with their start and end apart: 19 -> 0, of which waited for: 11 -> 0; matrix products, arithmetic and copies ran while one was open for 7% -> 0% of each run, Pallas kernels for 0% -> 0%
where the time goes in v2:
time: 478 us; the launch traced here: 472 us
  Pallas kernels  373 us (78%)
  matrix products  69.1 us (14%)
  local copies, waits for them, and re-layouts  20 us (4%)
  other arithmetic  8.63 us (2%)
    pallas_call x1, Pallas kernels, back(): pl.pallas_call(back_kernel, out_shape=shapes, in_specs=[vmem()] * 15 + [h...  151 us
    pallas_call x1, Pallas kernels, front(): pl.pallas_call(front_kernel, out_shape=shapes, in_specs=[vmem()] * 8 + [h...  116 us
    pallas_call x2, Pallas kernels, cube_sum(): pl.pallas_call(cube_sum_kernel, out_shape=jax.ShapeDtypeStruct((rows, col...  71.5 us
    pallas_call x1, Pallas kernels, cube_gather(): pl.pallas_call(cube_gather_kernel, out_shape=jax.ShapeDtypeStruct((8,) +...  34.3 us
    dot_general x3, matrix products, matmul_right_t(): lax.dot_general(left, right, (((1,), (1,)), ((), ())), preferred_element_...  25 us
    dot_general x3, matrix products, matmul(): return jnp.dot(left, right, preferred_element_type=jnp.float32)  24.2 us
    dot_general x3, matrix products, matmul_left_t(): lax.dot_general(left, right, (((0,), (0,)), ((), ())), preferred_element_...  19.9 us

profile of v2, /device:TPU:10, one launch (start us, length us, event | category | flops | bytes accessed | tf_op | source)
XLA Modules:
  0.0 471.7 jit_solution(4558136482654209449)
XLA Ops:
  0.6 1.5 copy.33.seg_col
  6.7 116.3 %front.1 = (bf16[1152,1536]{1,0:T(8,128)(2,1)}, bf16[1024,1152]{1,0:T(8,128)(2,1)}, bf16[2,1152,864]{2,1,0:T(8,128)(2,1)}, bf16[864,1152]{1,0:T(8,128)(2,1)}, bf...) custom-call(bf16[256,1152]{1,0:T(8,128)(2,1)} %tok.3, ...), custom_call_target="tpu_custom_call" | custom-call | tf_op jit(solution)/shard_map/front/pallas_call | solution.py:987
  123.0 7.8 %fusion.14 = f32[2048,864]{0,1:T(8,128)S(1)} fusion(bf16[2048,1152]{1,0:T(8,128)(2,1)} %bitcast.58, bf16[2,1152,864]{2,1,0:T(8,128)(2,1)} %get-tuple-element.39), kind=kOutput, calls=%fused_computation.25 | convolution fusion | flops 4076863488 | bytes 13860864 | tf_op jit(solution)/shard_map/dot_general | solution.py:64
  130.9 8.7 %multiply_convert_fusion.1 = (bf16[2048,864]{0,1:T(8,128)(2,1)S(1)}, f32[2048,864]{0,1:T(8,128)}) fusion(f32[2048,864]{0,1:T(8,128)S(1)} %fusion.14, bf16[2048,1152]{1,0:T(8,128)(2,1)S(1)} %bitcast.59, bf16[2,1152,864]{2,1,0:T(8,128)(2,1)S(1)} %copy-done.9), kind=kOutput, calls=%fused_computation.12 | convolution fusion | flops 4094558208 | bytes 24477696 | tf_op jit(solution)/shard_map/dot_general | solution.py:64
  139.6 7.7 %convolution_convert_fusion = bf16[2048,1152]{1,0:T(8,128)(2,1)} fusion(bf16[2048,864]{0,1:T(8,128)(2,1)S(1)} %get-tuple-element.75, bf16[864,1152]{1,0:T(8,128)(2,1)S(1)} %copy-done.11), kind=kOutput, calls=%fused_computation.3 | convolution fusion | flops 4079222784 | bytes 10248192 | tf_op jit(solution)/shard_map/dot_general | solution.py:64
  147.3 37.4 %cube_sum.2 = f32[256,1152]{1,0:T(8,128)} custom-call(bf16[8,256,1152]{2,1,0:T(8,128)(2,1)} %bitcast.53), custom_call_target="tpu_custom_call" | custom-call | tf_op jit(solution)/shard_map/cube_sum/pallas_call | solution.py:520
  184.8 1.4 multiply_reduce_fusion
  186.9 1.7 fusion.23
  188.6 2.9 fusion.24
  191.5 34.3 %cube_gather.1 = bf16[8,256,1152]{2,1,0:T(8,128)(2,1)} custom-call(bf16[256,1152]{1,0:T(8,128)(2,1)} %get-tuple-element.65.block), custom_call_target="tpu_custom_call" | custom-call | tf_op jit(solution)/shard_map/cube_gather/pallas_call | solution.py:461
  225.9 9.6 %convolution_convert_fusion.3.dn = bf16[864,1152]{1,0:T(8,128)(2,1)} fusion(bf16[2048,864]{0,1:T(8,128)(2,1)} %copy-done.13, bf16[2048,1152]{1,0:T(8,128)(2,1)} %bitcast.54), kind=kOutput, calls=%fused_computation.17 | convolution fusion | flops 4077858816 | bytes 10248192 | tf_op jit(solution)/shard_map/dot_general | solution.py:68
  235.4 12.0 %multiply_convert_fusion = (bf16[2048,864]{0,1:T(8,128)(2,1)S(1)}, bf16[2048,864]{0,1:T(8,128)(2,1)S(1)}) fusion(f32[2048,864]{0,1:T(8,128)} %copy-done.12, f32[2048,864]{0,1:T(8,128)} %get-tuple-element.76, bf16[2048,1152]{1,0:T(8,128)(2,1)S(1)} %bitcast.55, bf16[864,1152]{1,0:T(8,128)(2,1)S(1)} %copy-done.11), kind=kOutput, calls=%fused_computation.11 | convolution fusion | flops 4119330816 | bytes 27942912 | tf_op jit(solution)/shard_map/dot_general | solution.py:74
  247.4 5.2 %fusion.7 = bf16[1,1152,864]{2,1,0:T(8,128)(2,1)S(1)} fusion(bf16[2048,1152]{1,0:T(8,128)(2,1)S(1)} %bitcast.62, bf16[2048,864]{0,1:T(8,128)(2,1)S(1)} %get-tuple-element.62), kind=kOutput, calls=%fused_computation.18 | convolution fusion | flops 4077858816 | bytes 10248192 | tf_op jit(solution)/shard_map/dot_general | solution.py:68
  252.6 5.1 %fusion.8 = bf16[1,1152,864]{2,1,0:T(8,128)(2,1)S(1)} fusion(bf16[2048,1152]{1,0:T(8,128)(2,1)S(1)} %bitcast.63, bf16[2048,864]{0,1:T(8,128)(2,1)S(1)} %get-tuple-element.61), kind=kOutput, calls=%fused_computation.19 | convolution fusion | flops 4077858816 | bytes 10248192 | tf_op jit(solution)/shard_map/dot_general | solution.py:68
  257.8 2.6 pad_maximum_fusion.gu
  260.4 1.0 copy-done.10
  261.4 5.8 %fusion.12 = f32[2048,1152]{1,0:T(8,128)S(1)} fusion(bf16[2048,864]{0,1:T(8,128)(2,1)S(1)} %get-tuple-element.62, bf16[2,1152,864]{2,1,0:T(8,128)(2,1)S(1)} %copy-done.10), kind=kOutput, calls=%fused_computation.23 | convolution fusion | flops 4076863488 | bytes 15040512 | tf_op jit(solution)/shard_map/dot_general | solution.py:74
  267.2 7.2 %add_convert_fusion = bf16[2048,1152]{1,0:T(8,128)(2,1)} fusion(f32[2048,1152]{1,0:T(8,128)S(1)} %fusion.12, bf16[2048,864]{0,1:T(8,128)(2,1)S(1)} %get-tuple-element.61, bf16[2,1152,864]{2,1,0:T(8,128)(2,1)S(1)} %copy-done.10), kind=kOutput, calls=%fused_computation.2 | convolution fusion | flops 4081582080 | bytes 19759104 | tf_op jit(solution)/shard_map/dot_general | solution.py:74
  274.5 34.1 %cube_sum.3.d_normed = f32[256,1152]{1,0:T(8,128)} custom-call(bf16[8,256,1152]{2,1,0:T(8,128)(2,1)} %bitcast.52), custom_call_target="tpu_custom_call" | custom-call | tf_op jit(solution)/shard_map/cube_sum/pallas_call | solution.py:520
  309.2 150.5 %back.1 = (bf16[256,1152]{1,0:T(8,128)(2,1)}, f32[72,1536]{1,0:T(8,128)}, f32[64,1152]{1,0:T(8,128)}, f32[8,1152]{1,0:T(8,128)}, f32[2,72,6912]{2,1,0:T(8,128)}, /*index=5*/f32[432,1152]{1,0:T(8,128)}) custom-call(bf16[256,1152]{1,0:T(8,128)(2,1)} %tok.3, bf16[256,1152]{1,0:T(8,128)(2,1)} %d_out.1, f32[256,1152]{1,0:T(8,128)} %cube_sum.3.d_normed, ...), custom_call_target="tpu_custom_call" | custom-call | tf_op jit(solution)/shard_map/back/pallas_call | solution.py:1383
  459.7 1.1 fusion.33
  461.4 4.5 slice_bitcast_fusion
  468.5 0.8 copy.48
  470.0 1.3 copy.50
  (50 shorter events, 9.8 us)
Async XLA Ops:
  6.1 0.6 copy-start.7
  123.0 7.8 %copy-start.8 = (bf16[8,256,1152]{2,1,0:T(8,128)(2,1)S(1)}, bf16[8,256,1152]{2,1,0:T(8,128)(2,1)}, u32[]{:S(2)}) copy-start(bf16[8,256,1152]{2,1,0:T(8,128)(2,1)} %get-tuple-element.38) | copy-start | bytes 14155780
  123.0 7.8 %copy-start.9 = (bf16[2,1152,864]{2,1,0:T(8,128)(2,1)S(1)}, bf16[2,1152,864]{2,1,0:T(8,128)(2,1)}, u32[]{:S(2)}) copy-start(bf16[2,1152,864]{2,1,0:T(8,128)(2,1)} %get-tuple-element.39) | copy-start | bytes 11943940
  130.9 8.7 %copy-start.12 = (f32[2048,864]{0,1:T(8,128)}, f32[2048,864]{0,1:T(8,128)S(1)}, u32[]{:S(2)}) copy-start(f32[2048,864]{0,1:T(8,128)S(1)} %fusion.14) | copy-start | bytes 21233668
  130.9 8.7 %copy-start.11 = (bf16[864,1152]{1,0:T(8,128)(2,1)S(1)}, bf16[864,1152]{1,0:T(8,128)(2,1)}, u32[]{:S(2)}) copy-start(bf16[864,1152]{1,0:T(8,128)(2,1)} %get-tuple-element.40) | copy-start | bytes 5971972
  139.6 7.7 %copy-start.13 = (bf16[2048,864]{0,1:T(8,128)(2,1)}, bf16[2048,864]{0,1:T(8,128)(2,1)S(1)}, u32[]{:S(2)}) copy-start(bf16[2048,864]{0,1:T(8,128)(2,1)S(1)} %get-tuple-element.75) | copy-start | bytes 10616836
  147.3 39.6 %copy-start = (bf16[256,1152]{1,0:T(8,128)(2,1)S(1)}, bf16[256,1152]{1,0:T(8,128)(2,1)}, u32[]{:S(2)}) copy-start(bf16[256,1152]{1,0:T(8,128)(2,1)} %d_out.1) | copy-start | bytes 1769476
  147.3 41.3 %copy-start.1 = (f32[256,1152]{1,0:T(8,128)S(1)}, f32[256,1152]{1,0:T(8,128)}, u32[]{:S(2)}) copy-start(f32[256,1152]{1,0:T(8,128)} %get-tuple-element.37.h_mid) | copy-start | bytes 3538948
  225.8 9.6 %copy-start.2 = (bf16[8,256,1152]{2,1,0:T(8,128)(2,1)S(1)}, bf16[8,256,1152]{2,1,0:T(8,128)(2,1)}, u32[]{:S(2)}) copy-start(bf16[8,256,1152]{2,1,0:T(8,128)(2,1)} %cube_gather.1) | copy-start | bytes 14155780
  225.8 21.6 %slice-start = ((s8[4718592]{0:T(1024)(128)(4,1)}), s8[4194304]{0:T(1024)(128)(4,1)S(1)}, s32[]{:S(2)}) async-start(s8[4718592]{0:T(1024)(128)(4,1)} %bitcast.60), calls=%async_computation | async-start | bytes 8388608
  235.4 12.0 %slice-start.1 = ((s8[4718592]{0:T(1024)(128)(4,1)}), s8[524288]{0:T(1024)(128)(4,1)S(1)}, s32[]{:S(2)}) async-start(s8[4718592]{0:T(1024)(128)(4,1)} %bitcast.60), calls=%async_computation.1 | async-start | bytes 1048576
  257.8 3.7 copy-start.10
  459.7 7.4 %copy-start.5 = (f32[72,1536]{1,0:T(8,128)S(1)}, f32[72,1536]{1,0:T(8,128)}, u32[]{:S(2)}) copy-start(f32[72,1536]{1,0:T(8,128)} %get-tuple-element.54) | copy-start | bytes 1327108
  461.4 7.1 %copy-start.4 = (bf16[256,1152]{1,0:T(8,128)(2,1)S(1)}, bf16[256,1152]{1,0:T(8,128)(2,1)}, u32[]{:S(2)}) copy-start(bf16[256,1152]{1,0:T(8,128)(2,1)} %get-tuple-element.99) | copy-start | bytes 1769476
  461.4 7.9 %copy-start.6 = (f32[64,1152]{1,0:T(8,128)S(1)}, f32[64,1152]{1,0:T(8,128)}, u32[]{:S(2)}) copy-start(f32[64,1152]{1,0:T(8,128)} %get-tuple-element.103) | copy-start | bytes 884740
  461.4 8.6 %copy-start.3 = (f32[432,1152]{1,0:T(8,128)S(1)}, f32[432,1152]{1,0:T(8,128)}, u32[]{:S(2)}) copy-start(f32[432,1152]{1,0:T(8,128)} %get-tuple-element.110) | copy-start | bytes 5971972

commit v3 on v2

--- a/solution.py
+++ b/solution.py
@@ -446,94 +446,6 @@
     return ((0, first), (first, first), (2 * first, rows - 2 * first))
 
 
-def cube_gather_kernel(block, every, send, recv, local):
-    p = Place()
-    w = Wires(send, recv)
-    greet([p.cube(X), p.cube(Y), p.cube(Z)])
-    started = []
-    for _ in cube_gather_steps(p, w, block, every, local.at[0], started):
-        pass
-    for copy in started:
-        copy.wait_send()
-
-
-def cube_gather(block):
-    return pl.pallas_call(
-        cube_gather_kernel,
-        out_shape=jax.ShapeDtypeStruct((8,) + block.shape, block.dtype),
-        in_specs=[hbm()],
-        out_specs=hbm(),
-        scratch_shapes=sems(24) + [pltpu.SemaphoreType.DMA((1,))],
-        compiler_params=params(1),
-        name="cube_gather",
-    )(block)
-
-
-def cube_sum_kernel(parts, total, ready, third, second, first, send, recv):
-    p = Place()
-    w = Wires(send, recv)
-    near = {bit: p.cube(bit) for bit in (X, Y, Z)}
-    greet([near[X], near[Y], near[Z]])
-    started = []
-
-    def push(src, dst, bit):
-        copy = w.remote(src, dst, near[bit])
-        copy.start()
-        started.append(copy)
-        return copy
-
-    rows = total.shape[0]
-    half = rows // 2
-    far, mid, end = {}, {}, {}
-    for h in range(2):
-        for (start, size), link in zip(thirds(half), (X, Y, Z)):
-            at = pl.ds(h * half + start, size)
-            far[link, h] = push(parts.at[7, at], third.at[at], link)
-    for h in range(2):
-        for i, (link, onward, place) in enumerate(((X, Y, Y | Z), (Y, Z, X | Z), (Z, X, X | Y))):
-            start, size = thirds(half)[i]
-            at = pl.ds(h * half + start, size)
-            all_at = pl.ds(h * half, half)
-            far[link, h].wait_recv()
-            ready[i, all_at] = parts[place, all_at]
-            ready[i, at] = (parts[place, at].astype(F32) + third[at].astype(F32)).astype(BF16)
-            mid[onward, h] = push(ready.at[i, all_at], second.at[i, all_at], onward)
-    for h in range(2):
-        at = pl.ds(h * half, half)
-        for i, (came, place) in enumerate(((Y, Z), (Z, X), (X, Y))):
-            mid[came, h].wait_recv()
-            ready[3 + i, at] = (parts[place, at].astype(F32) + second[i, at].astype(F32)).astype(BF16)
-            end[place, h] = push(ready.at[3 + i, at], first.at[i, at], place)
-    for h in range(2):
-        at = pl.ds(h * half, half)
-        value = parts[0, at].astype(F32)
-        for i, place in enumerate((Z, X, Y)):
-            end[place, h].wait_recv()
-            value = value + first[i, at].astype(F32)
-        total[at, :] = value
-    for copy in started:
-        copy.wait_send()
-
-
-def cube_sum(parts):
-    _, rows, columns = parts.shape
-    return pl.pallas_call(
-        cube_sum_kernel,
-        out_shape=jax.ShapeDtypeStruct((rows, columns), F32),
-        in_specs=[vmem()],
-        out_specs=vmem(),
-        scratch_shapes=[
-            pltpu.VMEM((6, rows, columns), BF16),
-            pltpu.VMEM((rows, columns), BF16),
-            pltpu.VMEM((3, rows, columns), BF16),
-            pltpu.VMEM((3, rows, columns), BF16),
-        ]
-        + sems(24),
-        compiler_params=params(2),
-        name="cube_sum",
-    )(parts)
-
-
 def add(left, right):
     return (left.astype(F32) + right.astype(F32)).astype(BF16)
 
@@ -1391,6 +1303,285 @@
     )(tok, d_out, d_normed, gains_full, *saved, g_mpost, qkv_w, out_w, grad_gu, grad_dn)
 
 
+GELU_ROOT = math.sqrt(2.0 / math.pi)
+
+
+def gelu_parts(gate):
+    square = gate * gate
+    bend = jnp.tanh(GELU_ROOT * gate * (1.0 + 0.044715 * square))
+    half = 0.5 * (1.0 + bend)
+    slope = half + 0.5 * gate * (1.0 - bend * bend) * GELU_ROOT * (1.0 + 3 * 0.044715 * square)
+    return half * gate, slope
+
+
+def tiles(size, step):
+    return [slice(at, min(at + step, size)) for at in range(0, size, step)]
+
+
+class CubeSum:
+    MIDDLE = ((X, Y, Y | Z), (Y, Z, X | Z), (Z, X, X | Y))
+    NEAR = ((Y, Z), (Z, X), (X, Y))
+
+    def __init__(self, p, w, parts, third, second, first):
+        self.p, self.w, self.parts = p, w, parts
+        self.third, self.second, self.first = third, second, first
+        self.half = parts.shape[1] // 2
+        self.started = []
+        self.far, self.mid, self.end = {}, {}, {}
+
+    def push(self, src, dst, bit):
+        copy = self.w.remote(src, dst, self.p.cube(bit))
+        copy.start()
+        self.started.append(copy)
+        return copy
+
+    def send_far(self):
+        for h in range(2):
+            for (start, size), link in zip(thirds(self.half), (X, Y, Z)):
+                at = pl.ds(h * self.half + start, size)
+                self.far[link, h] = self.push(self.parts.at[7, at], self.third.at[at], link)
+
+    def send_middle(self):
+        for h in range(2):
+            for i, (link, onward, place) in enumerate(self.MIDDLE):
+                start, size = thirds(self.half)[i]
+                at = pl.ds(h * self.half + start, size)
+                all_at = pl.ds(h * self.half, self.half)
+                self.far[link, h].wait_recv()
+                self.parts[place, at] = add(self.parts[place, at], self.third[at, :])
+                self.mid[onward, h] = self.push(
+                    self.parts.at[place, all_at], self.second.at[i, all_at], onward
+                )
+
+    def send_near(self):
+        for h in range(2):
+            at = pl.ds(h * self.half, self.half)
+            for i, (came, place) in enumerate(self.NEAR):
+                self.mid[came, h].wait_recv()
+                self.parts[place, at] = add(self.parts[place, at], self.second[i, at])
+                self.end[place, h] = self.push(
+                    self.parts.at[place, at], self.first.at[i, at], place
+                )
+
+    def finish(self):
+        for h in range(2):
+            at = pl.ds(h * self.half, self.half)
+            value = self.parts[0, at].astype(F32)
+            for i, (_, place) in enumerate(self.NEAR):
+                self.end[place, h].wait_recv()
+                value = value + self.first[i, at].astype(F32)
+            yield at, value
+
+    def wait_sent(self):
+        for copy in self.started:
+            copy.wait_send()
+        self.started = []
+
+
+class CubeGather:
+    def __init__(self, p, w, block, every):
+        self.p, self.w, self.block, self.every = p, w, block, every
+        self.half = block.shape[0] // 2
+        self.started = []
+        self.near, self.middle, self.far = {}, {}, {}
+
+    def push(self, src, dst, bit):
+        copy = self.w.remote(src, dst, self.p.cube(bit))
+        copy.start()
+        self.started.append(copy)
+        return copy
+
+    def send_near(self, h):
+        at = pl.ds(h * self.half, self.half)
+        for bit in (X, Y, Z):
+            self.near[bit, h] = self.push(self.block.at[at], self.every.at[bit, at], bit)
+
+    def send_middle(self, h):
+        at = pl.ds(h * self.half, self.half)
+        for link, relay in ((X, Y), (Y, Z), (Z, X)):
+            self.near[relay, h].wait_recv()
+            self.middle[link | relay, h] = self.push(
+                self.every.at[relay, at], self.every.at[link | relay, at], link
+            )
+
+    def send_far(self, h):
+        for (start, size), link, relay in zip(thirds(self.half), (X, Y, Z), (Y | Z, X | Z, X | Y)):
+            at = pl.ds(h * self.half + start, size)
+            self.middle[relay, h].wait_recv()
+            self.far[link, h] = self.push(self.every.at[relay, at], self.every.at[7, at], link)
+
+    def wait_far(self):
+        for copy in self.far.values():
+            copy.wait_recv()
+
+    def wait_sent(self):
+        for copy in self.started:
+            copy.wait_send()
+        self.started = []
+
+
+def mlp_kernel(
+    every, gu, dn, h_mid, d_out, gains_full,
+    layer_out, d_normed, g_mpost, grad_gu, grad_dn,
+    m_all, wide_w, down_w, gate, up, hidden, dd_own, dd_all, parts, third, second, first,
+    send, recv, local,
+):
+    p = Place()
+    w = Wires(send, recv)
+    order = (7, 3, 5, 6, 4, 2, 1, 0)
+    loads = {r: pltpu.make_async_copy(every.at[r], m_all.at[r], local.at[r]) for r in order}
+    wide_load = pltpu.make_async_copy(gu, wide_w, local.at[8])
+    down_load = pltpu.make_async_copy(dn, down_w, local.at[9])
+    wide_load.start()
+    loads[7].start()
+    down_load.start()
+    for r in order[1:]:
+        loads[r].start()
+    greet([p.cube(X), p.cube(Y), p.cube(Z)])
+
+    length, width = m_all.shape[1:]
+    part = gate.shape[-1]
+    wide_tiles = tiles(part, 256)
+    down_tiles = tiles(width, 384)
+
+    def forward(r):
+        for at in wide_tiles:
+            g = jnp.dot(m_all[r], wide_w[0, :, at], preferred_element_type=F32)
+            u = jnp.dot(m_all[r], wide_w[1, :, at], preferred_element_type=F32)
+            gate[r, :, at] = g
+            up[r, :, at] = u
+            value, _ = gelu_parts(g)
+            hidden[r, :, at] = (value * u).astype(BF16)
+        for at in down_tiles:
+            parts[r, :, at] = jnp.dot(
+                hidden[r], down_w[:, at], preferred_element_type=F32
+            ).astype(BF16)
+
+    def backward(r):
+        for at in wide_tiles:
+            d_hidden = dot_columns(dd_all[r], down_w[at, :])
+            value, slope = gelu_parts(gate[r, :, at])
+            d_gate = d_hidden * up[r, :, at] * slope
+            gate[r, :, at] = d_gate.astype(BF16).astype(F32)
+            up[r, :, at] = (d_hidden * value).astype(BF16).astype(F32)
+        d_gate = gate[r].astype(BF16)
+        d_up = up[r].astype(BF16)
+        for at in down_tiles:
+            parts[r, :, at] = (
+                dot_columns(d_gate, wide_w[0, at, :]) + dot_columns(d_up, wide_w[1, at, :])
+            ).astype(BF16)
+
+    def several(step, places):
+        lax.fori_loop(0, 3, lambda i, _: (step(places(i)), 0)[1], 0)
+
+    def middles(i):
+        return 7 - lax.shift_right_logical(jnp.int32(4), i)
+
+    def nears(i):
+        return lax.shift_right_logical(jnp.int32(4), i)
+
+    total = CubeSum(p, w, parts, third, second, first)
+    wide_load.wait()
+    loads[7].wait()
+    down_load.wait()
+    forward(7)
+    total.send_far()
+    for r in order[1:]:
+        loads[r].wait()
+    several(forward, middles)
+    total.send_middle()
+    several(forward, nears)
+    total.send_near()
+    forward(0)
+
+    gather = CubeGather(p, w, dd_own, dd_all)
+    gain = gains_full[3]
+    g_rows = 0.0
+    for h, (at, value) in enumerate(total.finish()):
+        scale = norm_scale(value)
+        layer_out[at, :] = (h_mid[at, :] + value * scale * gain).astype(BF16)
+        d_value, g_part = norm_pull(value, scale, gain, d_out[at, :].astype(F32))
+        dd_own[at, :] = d_value.astype(BF16)
+        g_rows = g_rows + g_part
+        gather.send_near(h)
+    g_mpost[...] = g_rows
+    dd_all[0] = dd_own[...]
+    total.wait_sent()
+    backward(0)
+    gather.send_middle(0)
+    gather.send_middle(1)
+    several(backward, nears)
+    gather.send_far(0)
+    gather.send_far(1)
+    several(backward, middles)
+    gather.wait_far()
+    backward(7)
+
+    total = CubeSum(p, w, parts, third, second, first)
+    total.send_far()
+    grad_rows = 384
+
+    all_rows = 8 * length
+    for at in down_tiles:
+        grad_dn[:, at] = dot_rows(
+            hidden[...].reshape(all_rows, part), dd_all[:, :, at].reshape(all_rows, -1)
+        ).astype(BF16)
+    total.send_middle()
+    for matrix, held in ((0, gate), (1, up)):
+        hidden[...] = held[...].astype(BF16)
+
+        def grad_wide(i, _):
+            at = pl.ds(pl.multiple_of(i * grad_rows, 128), grad_rows)
+            left = m_all[:, :, at].reshape(all_rows, grad_rows)
+            grad_gu[matrix, at, :] = dot_rows(left, hidden[...].reshape(all_rows, part)).astype(BF16)
+            return 0
+
+        lax.fori_loop(0, width // grad_rows, grad_wide, 0)
+        if matrix == 0:
+            total.send_near()
+    for at, value in total.finish():
+        d_normed[at, :] = value
+    total.wait_sent()
+    gather.wait_sent()
+
+
+def mlp(every, gu, dn, h_mid, d_out, gains_full):
+    _, length, width = every.shape
+    part = dn.shape[0]
+    struct = jax.ShapeDtypeStruct
+    blocks = (8, length, width)
+    return pl.pallas_call(
+        mlp_kernel,
+        out_shape=(
+            struct((length, width), BF16),
+            struct((length, width), F32),
+            struct((1, width), F32),
+            struct(gu.shape, BF16),
+            struct(dn.shape, BF16),
+        ),
+        in_specs=[hbm()] * 3 + [vmem()] * 3,
+        out_specs=(vmem(),) * 5,
+        scratch_shapes=[
+            pltpu.VMEM(blocks, BF16),
+            pltpu.VMEM(gu.shape, BF16),
+            pltpu.VMEM(dn.shape, BF16),
+            pltpu.VMEM((8, length, part), F32),
+            pltpu.VMEM((8, length, part), F32),
+            pltpu.VMEM((8, length, part), BF16),
+            pltpu.VMEM((length, width), BF16),
+            pltpu.VMEM(blocks, BF16),
+            pltpu.VMEM(blocks, BF16),
+            pltpu.VMEM((length, width), BF16),
+            pltpu.VMEM((3, length, width), BF16),
+            pltpu.VMEM((3, length, width), BF16),
+        ]
+        + sems(64)
+        + [pltpu.SemaphoreType.DMA((10,))],
+        compiler_params=params(1),
+        name="mlp",
+    )(every, gu, dn, h_mid, d_out, gains_full)
+
+
 def pack_gains(vectors):
     rows = [jnp.pad(v, (0, 128 - v.shape[0])) for v in vectors]
     return jnp.concatenate(rows + [jnp.zeros(((8 - len(rows)) * 128,), F32)]).reshape(8, 128)
@@ -1410,34 +1601,12 @@
     ) = front(
         layer_in, segments, w_q, w_k, w_v, w_o, pack_gains(gain_list), w_gate, w_up, w_down, head
     )
-    gate_w, up_w = gu_w[0], gu_w[1]
-    m_all = m_all.reshape(-1, width)
-    gate_val = matmul(m_all, gate_w)
-    up_val = matmul(m_all, up_w)
-    hidden, pull_h = jax.vjp(gelu_product, gate_val, up_val)
-    h_low = to_low(hidden)
-    down_val = cube_sum(to_low(matmul(h_low, down_w)).reshape(8, -1, width))
-    post_mlp, pull_pm = jax.vjp(norm_rows, down_val, gains_full[3, 0])
-    layer_out = (h_mid + post_mlp).astype(BF16)
-
-    d_down, g_mpost = pull_pm(d_out.astype(F32))
-    dd_all = cube_gather(to_low(d_down)).reshape(-1, width)
-    grad_wdown = to_low(matmul_left_t(h_low, dd_all))
-    d_hidden = matmul_right_t(dd_all, down_w)
-    d_gate, d_up = pull_h(d_hidden)
-    d_gate_low = to_low(d_gate)
-    d_up_low = to_low(d_up)
-    grad_gu = jnp.stack(
-        [to_low(matmul_left_t(m_all, d_gate_low)), to_low(matmul_left_t(m_all, d_up_low))]
-    )
-    d_normed = cube_sum(
-        to_low(matmul_right_t(d_gate_low, gate_w) + matmul_right_t(d_up_low, up_w)).reshape(
-            8, -1, width
-        )
+    layer_out, d_normed, g_mpost, grad_gu, grad_wdown = mlp(
+        m_all, gu_w, down_w, h_mid, d_out, gains_full
     )
     saved = (a_low, qk_proj, q_low, k_low, v_low, probs, o_low, attn_proj, h_mid, tables)
     grad_x, grad_qkv, grad_out, grad_gains, grad_gu, grad_dn = back(
-        layer_in, d_out, d_normed, gains_full, saved, g_mpost[None], qkv_w, out_w, grad_gu,
+        layer_in, d_out, d_normed, gains_full, saved, g_mpost, qkv_w, out_w, grad_gu,
         grad_wdown, rows, w_o.shape[0],
     )
     shard = lax.axis_index("fsdp")

time: 478 us -> 419 us (0.88)
  matrix products: 69.1 us -> 0 us
  Pallas kernels: 373 us -> 389 us
  other arithmetic: 8.63 us -> 0.01 us
    dot_general x9 -> x0, matrix products: 69.1 us -> none  [the longest x3 25 us: matmul_right_t(): lax.dot_general(left, right, (((1,), (1,)), ((), ())), preferred_element_...]
    pallas_call x3 -> x1, Pallas kernels: 106 us -> 122 us  [mlp(): pl.pallas_call(mlp_kernel, out_shape=(struct((length, width), BF16), stru...]
where the time goes in v3:
time: 419 us; the launch traced here: 411 us
  Pallas kernels  389 us (93%)
  local copies, waits for them, and re-layouts  20.3 us (5%)
    pallas_call x1, Pallas kernels, back(): pl.pallas_call(back_kernel, out_shape=shapes, in_specs=[vmem()] * 15 + [h...  151 us
    pallas_call x1, Pallas kernels, mlp(): pl.pallas_call(mlp_kernel, out_shape=(struct((length, width), BF16), stru...  122 us
    pallas_call x1, Pallas kernels, front(): pl.pallas_call(front_kernel, out_shape=shapes, in_specs=[vmem()] * 8 + [h...  116 us

profile of v3, /device:TPU:10, one launch (start us, length us, event | category | flops | bytes accessed | tf_op | source)
XLA Modules:
  0.0 410.6 jit_solution(8087034499212125705)
XLA Ops:
  0.6 1.5 copy.31.seg_col
  2.1 0.7 constant_dynamic-update-slice_fusion.6
  2.8 0.7 constant_dynamic-update-slice_fusion.5
  3.4 0.7 constant_dynamic-update-slice_fusion.4
  4.1 0.7 constant_dynamic-update-slice_fusion.3
  4.8 0.7 constant_dynamic-update-slice_fusion.2
  5.4 0.7 constant_dynamic-update-slice_fusion.1
  6.1 0.6 copy-done.4
  6.7 116.3 %front.1 = (bf16[1152,1536]{1,0:T(8,128)(2,1)}, bf16[1024,1152]{1,0:T(8,128)(2,1)}, bf16[2,1152,864]{2,1,0:T(8,128)(2,1)}, bf16[864,1152]{1,0:T(8,128)(2,1)}, bf...) custom-call(bf16[256,1152]{1,0:T(8,128)(2,1)} %tok.3, ...), custom_call_target="tpu_custom_call" | custom-call | tf_op jit(solution)/shard_map/front/pallas_call | solution.py:899
  123.0 121.9 %mlp.1 = (bf16[256,1152]{1,0:T(8,128)(2,1)}, f32[256,1152]{1,0:T(8,128)}, f32[1,1152]{1,0:T(1,128)}, bf16[2,1152,864]{2,1,0:T(8,128)(2,1)}, bf16[864,1152]{1,0:T(8,128)(2,1)}) custom-call(bf16[8,256,1152]{2,1,0:T(8,128)(2,1)} %get-tuple-element.42.every, bf16[2,1152,864]{2,1,0:T(8,128)(2,1)} %get-tuple-element.43.gu, ...), custom_call_target="tpu_custom_call" | custom-call | tf_op jit(solution)/shard_map/mlp/pallas_call | solution.py:1553
  244.9 151.1 %back.1 = (bf16[256,1152]{1,0:T(8,128)(2,1)}, f32[72,1536]{1,0:T(8,128)}, f32[64,1152]{1,0:T(8,128)}, f32[8,1152]{1,0:T(8,128)}, f32[2,72,6912]{2,1,0:T(8,128)}, /*index=5*/f32[432,1152]{1,0:T(8,128)}) custom-call(bf16[256,1152]{1,0:T(8,128)(2,1)} %tok.3, bf16[256,1152]{1,0:T(8,128)(2,1)} %d_out.3, f32[256,1152]{1,0:T(8,128)} %get-tuple-element.48.d_normed, ...), custom_call_target="tpu_custom_call" | custom-call | tf_op jit(solution)/shard_map/back/pallas_call | solution.py:1295
  396.0 1.1 fusion.7
  397.1 0.6 fusion.4
  397.7 4.4 %slice_bitcast_fusion = (f32[72,6912]{1,0:T(8,128)}, f32[72,6912]{1,0:T(8,128)}) fusion(f32[2,72,6912]{2,1,0:T(8,128)} %get-tuple-element.67), kind=kLoop, calls=%fused_computation | loop fusion | bytes 7962624 | tf_op jit(solution)/shard_map/squeeze | solution.py:1629
  402.2 0.6 fusion.2
  402.8 0.6 fusion
  403.3 1.7 slice.33
  405.0 1.6 fusion.6
  406.6 0.0 copy-done.1
  406.6 0.8 copy.43
  407.4 0.0 copy-done.2
  407.4 0.8 copy.44
  408.3 0.7 copy.45
  409.0 1.3 copy.46
  (9 shorter events, 0.0 us)
Async XLA Ops:
  6.1 0.6 copy-start.4
  397.7 8.9 %copy-start.1 = (bf16[256,1152]{1,0:T(8,128)(2,1)S(1)}, bf16[256,1152]{1,0:T(8,128)(2,1)}, u32[]{:S(2)}) copy-start(bf16[256,1152]{1,0:T(8,128)(2,1)} %get-tuple-element.100) | copy-start | bytes 1769476
  397.7 9.7 %copy-start.2 = (bf16[256,1152]{1,0:T(8,128)(2,1)S(1)}, bf16[256,1152]{1,0:T(8,128)(2,1)}, u32[]{:S(2)}) copy-start(bf16[256,1152]{1,0:T(8,128)(2,1)} %get-tuple-element.101) | copy-start | bytes 1769476
  402.2 6.1 %copy-start.3 = (f32[64,1152]{1,0:T(8,128)S(1)}, f32[64,1152]{1,0:T(8,128)}, u32[]{:S(2)}) copy-start(f32[64,1152]{1,0:T(8,128)} %get-tuple-element.105) | copy-start | bytes 884740
  402.2 6.8 %copy-start = (f32[432,1152]{1,0:T(8,128)S(1)}, f32[432,1152]{1,0:T(8,128)}, u32[]{:S(2)}) copy-start(f32[432,1152]{1,0:T(8,128)} %get-tuple-element.112) | copy-start | bytes 5971972
